TPU v7x, 128 devices: a whole 4x4x4 slice. The times are simulated.
128 devices in a mesh: ctx: 64 (over y_hi, z, x, core), shard: 2 (over y_lo).
Axes of the slice: x: 4, y: 4 (y_hi: 2, y_lo: 2; y = y_hi * 2 + y_lo), z: 4, core: 2. Of those that a mesh axis runs over, the one named last changes fastest.
Arguments:
- hidden_in: float32 [8192, 1152], P('ctx'), may hold values from -6 to 6
- out_grad: float32 [8192, 1152], P('ctx'), may hold values from -16 to 16
- block_order: int32 [64], replicated, may hold values from 0 to 63, each once
- norm_gains: float32 [4, 1152], replicated, may hold values from 0.1 to 1.9
- head_gains: float32 [2, 256], replicated, may hold values from 0.1 to 1.9
- w_query: bfloat16 [1152, 1024], P('ctx', 'shard'), may hold values from -0.1875 to 0.1875
- w_key: bfloat16 [1152, 256], P('ctx'), may hold values from -0.1875 to 0.1875
- w_value: bfloat16 [1152, 256], P('ctx'), may hold values from -0.1875 to 0.1875
- w_out: bfloat16 [1024, 1152], P('shard', 'ctx'), may hold values from -0.1875 to 0.1875
- w_gate: bfloat16 [1152, 6912], P('ctx', 'shard'), may hold values from -0.1875 to 0.1875
- w_up: bfloat16 [1152, 6912], P('ctx', 'shard'), may hold values from -0.1875 to 0.1875
- w_down: bfloat16 [6912, 1152], P('shard', 'ctx'), may hold values from -0.078125 to 0.078125
Outputs:
- block_out: float32 [8192, 1152], P('ctx')
- input_grad: float32 [8192, 1152], P('ctx')
- query_wgrad: float32 [1152, 1024], P('ctx', 'shard')
- key_wgrad: float32 [1152, 256], P('ctx')
- value_wgrad: float32 [1152, 256], P('ctx')
- out_wgrad: float32 [1024, 1152], P('shard', 'ctx')
- gate_wgrad: float32 [1152, 6912], P('ctx', 'shard')
- up_wgrad: float32 [1152, 6912], P('ctx', 'shard')
- down_wgrad: float32 [6912, 1152], P('shard', 'ctx')
- norm_grads: float32 [4, 1152], P(None, 'ctx')
- head_grads: float32 [2, 256], P(None, 'ctx')
Inputs may be any that keep to these rules, and one draw needn't show every extreme that they name: The i-th device of ctx holds sequence block block_order[i] of 128 positions; every block appears once.
All inputs are finite; a program needn't handle non-finite values.
Results may differ from a plain program's by a relative error of at most 0.04.
Values may be sent and summed in bfloat16 or wider, within the bound.
No kernel may reach another device: no remote copies, remote signals or barrier semaphores. Data moves between devices by JAX's collectives and lax.ppermute only.
A program may use at most 256 MiB of HBM per device.

v0:
```python
import math

import jax
import jax.numpy as jnp
from jax import lax
from jax.sharding import PartitionSpec as P

HD = 256


EPS = 1e-06
THETA = 1000000.0
NEG = -1e30


def matmul(left, right):
    return jnp.dot(left, right, preferred_element_type=jnp.float32)


def inner_rows(left, right):
    return lax.dot_general(
        left, right, (((0,), (0,)), ((), ())), preferred_element_type=jnp.float32
    )


def inner_cols(left, right):
    return lax.dot_general(
        left, right, (((1,), (1,)), ((), ())), preferred_element_type=jnp.float32
    )


def rms_scale(values, gain):
    return values * lax.rsqrt(jnp.mean(values * values, axis=-1, keepdims=True) + EPS) * gain


def rotate(values, cosine_table, sine_table):
    half_width = values.shape[-1] // 2
    first = values[..., :half_width]
    second = values[..., half_width:]
    return jnp.concatenate(
        [first * cosine_table - second * sine_table, second * cosine_table + first * sine_table],
        axis=-1,
    )


def head_path(values, gain, cosine_table, sine_table):
    return rotate(rms_scale(values, gain), cosine_table, sine_table)


def geglu(gate_pre, up_pre):
    return jax.nn.gelu(gate_pre, approximate=True) * up_pre


def tables(positions, head_width):
    frequency = jnp.arange(head_width // 2, dtype=jnp.float32)
    inverse = jnp.exp(frequency * (-2.0 * math.log(THETA) / head_width))
    angles = positions.astype(jnp.float32)[:, None] * inverse[None, :]
    return (jnp.cos(angles), jnp.sin(angles))


def probabilities(queries, query_pos, keys, key_pos, log_sums, score_scale):
    scores = inner_cols(queries, keys) * score_scale
    allowed = query_pos[:, None] >= key_pos[None, :]
    return jnp.where(allowed, jnp.exp(jnp.where(allowed, scores, NEG) - log_sums[:, None]), 0.0)


def unchanged(state):
    return state


def shards(
    hidden_in,
    out_grad,
    block_order,
    norm_gains,
    head_gains,
    w_query,
    w_key,
    w_value,
    w_out,
    w_gate,
    w_up,
    w_down,
):
    query_full, key_full, value_full, out_full, gate_full, up_full, down_full = (
        lax.all_gather(w_query, "ctx", axis=0, tiled=True),
        lax.all_gather(w_key, "ctx", axis=0, tiled=True),
        lax.all_gather(w_value, "ctx", axis=0, tiled=True),
        lax.all_gather(w_out, "ctx", axis=1, tiled=True),
        lax.all_gather(w_gate, "ctx", axis=0, tiled=True),
        lax.all_gather(w_up, "ctx", axis=0, tiled=True),
        lax.all_gather(w_down, "ctx", axis=1, tiled=True),
    )
    tokens = hidden_in.shape[0]
    head_width = HD
    local_heads = query_full.shape[1] // head_width
    rows = tokens * local_heads
    ctx_count = lax.axis_size("ctx")
    device = lax.axis_index("ctx")
    score_scale = head_width ** (-0.5)
    offsets = jnp.arange(tokens, dtype=jnp.int32)
    all_pos = (block_order[:, None] * tokens + offsets[None, :]).reshape(-1)
    own_pos = lax.dynamic_slice_in_dim(all_pos, device * tokens, tokens)
    own_rows_pos = jnp.repeat(own_pos, local_heads)
    own_last = jnp.max(own_pos)
    cosine_table, sine_table = tables(own_pos, head_width)
    attn_val, pre_attn_back = jax.vjp(rms_scale, hidden_in, norm_gains[0])
    attn_low = attn_val.astype(jnp.bfloat16)
    query_pre = matmul(attn_low, query_full).reshape(tokens, local_heads, head_width)
    key_pre = matmul(attn_low, key_full)
    value_low = matmul(attn_low, value_full).astype(jnp.bfloat16)
    query_val, query_back = jax.vjp(
        lambda values, gain: head_path(
            values, gain, cosine_table[:, None, :], sine_table[:, None, :]
        ),
        query_pre,
        head_gains[0],
    )
    key_val, key_back = jax.vjp(
        lambda values, gain: head_path(values, gain, cosine_table, sine_table),
        key_pre,
        head_gains[1],
    )
    query_rows = query_val.astype(jnp.bfloat16).reshape(rows, head_width)
    key_low = key_val.astype(jnp.bfloat16)
    start_state = (
        jnp.full((rows,), NEG, jnp.float32),
        jnp.zeros((rows,), jnp.float32),
        jnp.zeros((rows, head_width), jnp.float32),
    )
    keys = lax.all_gather(key_low, "ctx", axis=0, tiled=True)
    values = lax.all_gather(value_low, "ctx", axis=0, tiled=True)

    def attend_update(state):
        best, total, accum = state
        scores = inner_cols(query_rows, keys) * score_scale
        allowed = own_rows_pos[:, None] >= all_pos[None, :]
        scores = jnp.where(allowed, scores, NEG)
        newest = jnp.maximum(best, jnp.max(scores, axis=1))
        weights = jnp.where(allowed, jnp.exp(scores - newest[:, None]), 0.0)
        total = jnp.sum(weights, axis=1)
        accum = matmul(weights.astype(jnp.bfloat16), values)
        return (newest, total, accum)

    best, total, accum = lax.cond(
        jnp.min(all_pos) <= own_last, attend_update, unchanged, start_state
    )
    attn_rows = accum / total[:, None]
    log_total = best + jnp.log(total)
    attn_flat = attn_rows.astype(jnp.bfloat16).reshape(tokens, local_heads * head_width)
    attn_out = lax.psum(matmul(attn_flat, out_full).astype(jnp.bfloat16), "shard").astype(
        jnp.float32
    )
    post_attn, post_attn_back = jax.vjp(rms_scale, attn_out, norm_gains[1])
    mid_state = hidden_in + post_attn
    ffn_val, ffn_norm_back = jax.vjp(rms_scale, mid_state, norm_gains[2])
    ffn_low = ffn_val.astype(jnp.bfloat16)
    gate_pre = matmul(ffn_low, gate_full)
    up_pre = matmul(ffn_low, up_full)
    hidden_val, geglu_back = jax.vjp(geglu, gate_pre, up_pre)
    hidden_low = hidden_val.astype(jnp.bfloat16)
    ffn_out = lax.psum(matmul(hidden_low, down_full).astype(jnp.bfloat16), "shard").astype(
        jnp.float32
    )
    post_ffn, post_ffn_back = jax.vjp(rms_scale, ffn_out, norm_gains[3])
    block_out = mid_state + post_ffn
    ffn_grad, gain_four = post_ffn_back(out_grad)
    ffn_grad_low = ffn_grad.astype(jnp.bfloat16)
    hidden_grad = inner_cols(ffn_grad_low, down_full)
    gate_grad, up_grad = geglu_back(hidden_grad)
    gate_low = gate_grad.astype(jnp.bfloat16)
    up_low = up_grad.astype(jnp.bfloat16)
    down_wgrad = inner_rows(hidden_low, ffn_grad_low)
    gate_wgrad = inner_rows(ffn_low, gate_low)
    up_wgrad = inner_rows(ffn_low, up_low)
    ffn_norm_grad = lax.psum(
        (inner_cols(gate_low, gate_full) + inner_cols(up_low, up_full)).astype(jnp.bfloat16),
        "shard",
    ).astype(jnp.float32)
    mid_from, gain_three = ffn_norm_back(ffn_norm_grad)
    mid_grad = out_grad + mid_from
    attn_grad, gain_two = post_attn_back(mid_grad)
    attn_grad_low = attn_grad.astype(jnp.bfloat16)
    out_wgrad = inner_rows(attn_flat, attn_grad_low)
    rows_grad = inner_cols(attn_grad_low, out_full).astype(jnp.bfloat16).reshape(rows, head_width)
    row_dot = jnp.sum(rows_grad.astype(jnp.float32) * attn_rows, axis=1)
    zero_query = jnp.zeros((rows, head_width), jnp.float32)
    fold_start = (zero_query, jnp.zeros((tokens * ctx_count, 2 * head_width), jnp.float32))
    back_keys = lax.all_gather(key_low, "ctx", axis=0, tiled=True)
    back_values = lax.all_gather(value_low, "ctx", axis=0, tiled=True)

    def back_update(state):
        probs = probabilities(query_rows, own_rows_pos, back_keys, all_pos, log_total, score_scale)
        prob_grad = inner_cols(rows_grad, back_values)
        score_grad = (probs * (prob_grad - row_dot[:, None])).astype(jnp.bfloat16)
        query_acc = matmul(score_grad, back_keys) * score_scale
        key_piece = inner_rows(score_grad, query_rows) * score_scale
        value_piece = inner_rows(probs.astype(jnp.bfloat16), rows_grad)
        joined = jnp.concatenate([key_piece, value_piece], axis=1)
        result = (query_acc, joined)
        return result

    folded = lax.cond(jnp.min(all_pos) <= own_last, back_update, unchanged, fold_start)
    query_grad = folded[0]
    pair_grad = lax.psum_scatter(folded[1], "ctx", scatter_dimension=0, tiled=True)
    query_pre_grad, query_gain_part = query_back(
        query_grad.reshape(tokens, local_heads, head_width)
    )
    query_pre_low = query_pre_grad.astype(jnp.bfloat16).reshape(tokens, local_heads * head_width)
    query_wgrad = inner_rows(attn_low, query_pre_low)
    attn_norm_part = inner_cols(query_pre_low, query_full)
    attn_norm_sum, pair_sum, query_gain = (
        lax.psum(attn_norm_part.astype(jnp.bfloat16), "shard").astype(jnp.float32),
        lax.psum(pair_grad.astype(jnp.bfloat16), "shard").astype(jnp.float32),
        lax.psum(query_gain_part.astype(jnp.bfloat16), "shard").astype(jnp.float32),
    )
    key_pre_grad, key_gain = key_back(pair_sum[:, :head_width])
    key_pre_low = key_pre_grad.astype(jnp.bfloat16)
    value_grad_low = pair_sum[:, head_width:].astype(jnp.bfloat16)
    key_wgrad = inner_rows(attn_low, key_pre_low)
    value_wgrad = inner_rows(attn_low, value_grad_low)
    attn_norm_grad = (
        attn_norm_sum + inner_cols(key_pre_low, key_full) + inner_cols(value_grad_low, value_full)
    )
    input_from, gain_one = pre_attn_back(attn_norm_grad)
    input_grad = mid_grad + input_from
    norm_grads = jnp.stack([gain_one, gain_two, gain_three, gain_four])
    head_grads = jnp.stack([query_gain, key_gain])
    summed = (
        lax.psum_scatter(query_wgrad, "ctx", scatter_dimension=0, tiled=True),
        lax.psum_scatter(key_wgrad, "ctx", scatter_dimension=0, tiled=True),
        lax.psum_scatter(value_wgrad, "ctx", scatter_dimension=0, tiled=True),
        lax.psum_scatter(out_wgrad, "ctx", scatter_dimension=1, tiled=True),
        lax.psum_scatter(gate_wgrad, "ctx", scatter_dimension=0, tiled=True),
        lax.psum_scatter(up_wgrad, "ctx", scatter_dimension=0, tiled=True),
        lax.psum_scatter(down_wgrad, "ctx", scatter_dimension=1, tiled=True),
        lax.psum_scatter(norm_grads, "ctx", scatter_dimension=1, tiled=True),
        lax.psum_scatter(head_grads, "ctx", scatter_dimension=1, tiled=True),
    )
    result = (
        block_out,
        input_grad,
        summed[0],
        summed[1],
        summed[2],
        summed[3],
        summed[4],
        summed[5],
        summed[6],
        summed[7],
        summed[8],
    )
    return result


def solution(mesh):
    placed = (
        P("ctx", None),
        P("ctx", None),
        P(),
        P(),
        P(),
        P("ctx", "shard"),
        P("ctx", None),
        P("ctx", None),
        P("shard", "ctx"),
        P("ctx", "shard"),
        P("ctx", "shard"),
        P("shard", "ctx"),
    )
    return jax.shard_map(
        shards,
        mesh=mesh,
        in_specs=placed,
        out_specs=(
            P("ctx", None),
            P("ctx", None),
            P("ctx", "shard"),
            P("ctx", None),
            P("ctx", None),
            P("shard", "ctx"),
            P("ctx", "shard"),
            P("ctx", "shard"),
            P("shard", "ctx"),
            P(None, "ctx"),
            P(None, "ctx"),
        ),
        check_vma=False,
    )
```

profile of v0, /device:TPU:1, one launch (start us, length us, event | category | flops | bytes accessed | tf_op | source)
XLA Modules:
  0.0 1952.2 jit_solution(9479599536240235386)
XLA Ops:
  10.1 100.9 %all-gather.1 = bf16[64,18,256]{2,1,0:T(8,128)(2,1)S(1)} all-gather(bf16[1,18,256]{2,1,0:T(8,128)(2,1)} %bitcast.112), channel_id=1, replica_groups=mesh['ctx'=64,'shard'=2] {'ctx'}, dimensions={0}, use_global_device_ids=true | all-gather | bytes 599040 | tf_op jit(solution)/shard_map/all_gather | solution.py:87
  116.8 90.9 %all-gather.2 = bf16[64,18,256]{2,1,0:T(8,128)(2,1)S(1)} all-gather(bf16[1,18,256]{2,1,0:T(8,128)(2,1)S(1)} %bitcast.113), channel_id=1, replica_groups=mesh['ctx'=64,'shard'=2] {'ctx'}, dimensions={0}, use_global_device_ids=true | all-gather | bytes 599040 | tf_op jit(solution)/shard_map/all_gather | solution.py:88
  221.3 72.5 %all-gather.17.cloned.1.call-done = bf16[8192,256]{1,0:T(8,128)(2,1)} async-done(((bf16[128,256]{1,0:T(8,128)(2,1)}), bf16[8192,256]{1,0:T(8,128)(2,1)}) %all-gather.17.cloned.1.call-update) | async-done | bytes 4194320 | tf_op jit(solution)/shard_map/all_gather | solution.py:132
  293.9 11.0 conditional.2
  294.1 3.9 fusion.82
  311.5 23.9 %all-reduce.27.cloned.1.call-done = bf16[128,1152]{1,0:T(8,128)(2,1)} async-done(((bf16[128,1152]{1,0:T(8,128)(2,1)}), bf16[128,1152]{1,0:T(8,128)(2,1)}) %all-reduce.27.cloned.1.call-update) | async-done | bytes 294928 | tf_op jit(solution)/shard_map/psum | solution.py:151
  337.9 90.5 %all-gather.23.cloned.1.call-done = bf16[64,18,3456]{2,1,0:T(8,128)(2,1)} async-done(((bf16[1,18,3456]{2,1,0:T(8,128)(2,1)}), bf16[64,18,3456]{2,1,0:T(8,128)(2,1)}) %all-gather.23.cloned.1.call-update) | async-done | bytes 7962640 | tf_op jit(solution)/shard_map/all_gather | solution.py:90
  428.4 13.2 reshape.257
  441.6 75.8 %all-gather.25.cloned.1.call-done = bf16[64,18,3456]{2,1,0:T(8,128)(2,1)} async-done(((bf16[1,18,3456]{2,1,0:T(8,128)(2,1)}), bf16[64,18,3456]{2,1,0:T(8,128)(2,1)}) %all-gather.25.cloned.1.call-update) | async-done | bytes 7962640 | tf_op jit(solution)/shard_map/all_gather | solution.py:91
  517.4 13.2 reshape.259
  530.6 4.8 fusion.86
  539.5 66.9 %all-gather.27.cloned.1.call-done = bf16[64,18,3456]{2,1,0:T(8,128)(2,1)} async-done(((bf16[1,18,3456]{2,1,0:T(8,128)(2,1)}), bf16[64,18,3456]{2,1,0:T(8,128)(2,1)}) %all-gather.27.cloned.1.call-update) | async-done | bytes 7962640 | tf_op jit(solution)/shard_map/all_gather | solution.py:92
  606.4 13.2 reshape.261
  619.6 6.4 convolution_convert_fusion
  626.1 27.1 %all-reduce.29.cloned.1.call-done = bf16[128,1152]{1,0:T(8,128)(2,1)} async-done(((bf16[128,1152]{1,0:T(8,128)(2,1)}), bf16[128,1152]{1,0:T(8,128)(2,1)}) %all-reduce.29.cloned.1.call-update) | async-done | bytes 294928 | tf_op jit(solution)/shard_map/psum | solution.py:162
  657.2 7.3 multiply_convert_fusion
  670.4 31.4 %all-reduce.31.cloned.1.call-done = bf16[128,1152]{1,0:T(8,128)(2,1)} async-done(((bf16[128,1152]{1,0:T(8,128)(2,1)}), bf16[128,1152]{1,0:T(8,128)(2,1)}) %all-reduce.31.cloned.1.call-update) | async-done | bytes 294928 | tf_op jit(solution)/shard_map/psum | solution.py:176
  708.9 22.7 %conditional.3 = (f32[8192,512]{0,1:T(8,128)}, f32[128,2,128]{2,1,0:T(2,128)S(1)}, f32[128,2,128]{2,1,0:T(2,128)S(1)}, f32[128,2,128]{2,1,0:T(2,128)S(1)}) conditional(s32[]{:T(128)} %convert_element_type.100, () %tuple.37, (s32[128,2]{1,0:T(8,128)S(1)}, s32[64,128]{1,0:T(8,128)S(1)}, bf16[256,256]{1,0:T(8,128)(2,1)}, bf16[8192,256]{1,0:T(8,128)(2,1)}, ...), branch_computations={%region_18.19_spmd, %region_19.0_spmd} | conditional | flops 5394169856 | bytes 121152600 | solution.py:203
  710.3 4.3 compare_select_fusion.1
  721.8 6.6 pad_maximum_fusion
  731.6 17.6 copy.33
  750.4 7.8 fusion.91
  758.2 7.7 fusion.92
  768.4 335.2 %reduce-scatter.12.cloned.1.call-done = f32[128,512]{1,0:T(8,128)} async-done(((f32[8192,512]{1,0:T(8,128)}), f32[128,512]{1,0:T(8,128)}) %reduce-scatter.12.cloned.1.call-update) | async-done | bytes 262160 | tf_op jit(solution)/shard_map/reduce_scatter | solution.py:205
  1105.4 8.9 fusion.93
  1118.2 23.8 %all-reduce.35.cloned.1.call-done = (bf16[128,512]{1,0:T(8,128)(2,1)}, bf16[128,1152]{1,0:T(8,128)(2,1)}) async-done(((bf16[128,512]{1,0:T(8,128)(2,1)}, bf16[128,1152]{1,0:T(8,128)(2,1)}), (bf16[128,512]{1,0:T(8,128)(2,1)}, bf16[128,1152]{1,0:T(8,128)(2,1)})) %all-reduce.35.cloned.1.call-update) | async-done | bytes 426000 | tf_op jit(solution)/shard_map/psum | solution.py:214
  1147.7 197.1 %fusion.76 = (f32[24,512]{1,0:T(8,128)S(1)}, f32[24,256]{1,0:T(8,128)S(1)}, f32[24,256]{1,0:T(8,128)S(1)}, f32[512,24]{0,1:T(8,128)S(1)}) fusion(f32[1152,512]{1,0:T(8,128)} %fusion.88, f32[1152,256]{1,0:T(8,128)} %fusion.89, f32[1152,256]{1,0:T(8,128)} %fusion.65, f32[512,1152]{0,1:T(8,128)} %fusion.90), kind=kCustom, calls=%all-reduce-scatter.4 | all-reduce-scatter fusion | flops 2359297 | bytes 7225856
  1348.2 13.9 collective-permute-start.31
  1371.0 8.3 collective-permute-start.25
  1384.2 3.7 collective-permute-start.21
  1397.1 4.2 psum.47
  1401.3 4.5 collective-permute-start.18
  1409.7 5.1 collective-permute-start.46
  1418.5 5.2 collective-permute-start.44
  1425.7 4.6 collective-permute-start.42
  1437.2 3.7 collective-permute-start.37
  1446.0 5.5 collective-permute-start.34
  1459.8 5.0 collective-permute-start.14
  1483.1 9.2 collective-permute-start.6
  1495.8 316.0 %all-reduce.17 = (f32[4,1152]{1,0:T(4,128)S(1)}, f32[2,256]{1,0:T(2,128)S(1)}) all-reduce(f32[4,1152]{1,0:T(4,128)S(1)} %pad_maximum_fusion.3, f32[2,256]{1,0:T(2,128)S(1)} %pad_maximum_fusion.4), channel_id=10, replica_groups=mesh['ctx'=64,'shard'=2] {'ctx'}, use_global_device_ids=true, to_apply=%region_38.39.clone | all-reduce | flops 5120 | bytes 40960
  1817.1 4.2 collective-permute-start
  1821.9 14.1 collective-permute-start.62
  1836.1 5.1 collective-permute-start.61
  1847.5 4.2 collective-permute-start.58
  1852.4 4.1 concatenate.23
  1870.2 15.9 collective-permute-start.52
  1886.2 3.7 collective-permute-start.51
  1904.4 37.2 %all-reduce.33.cloned.1.call-done = (f32[1152,3456]{1,0:T(8,128)}, f32[1152,3456]{1,0:T(8,128)}, f32[3456,1152]{0,1:T(8,128)}) async-done(((f32[1152,3456]{1,0:T(8,128)}, f32[1152,3456]{1,0:T(8,128)}, f32[3456,1152]{0,1:T(8,128)}), (f32[1152,3456]{1,0:T(8,128)}, f32[1152,3456]{1,0:T(8,128)}, f32[3456,1152]{0,1:T(8,128)})) %all-reduce.33.cloned.1.call-update) | async-done | bytes 47775760
  (397 shorter events, 203.7 us)
Async XLA Ops:
  7.2 203.6 %all-gather.19.cloned.1.call-start = ((), (), s32[]{:S(2)}) async-start(), calls=%async_computation.7 | async-start | bytes 1597440 | tf_op jit(solution)/shard_map/all_gather | solution.py:86
  7.9 206.2 %all-gather.21.cloned.1.call-start = ((), (), s32[]{:S(2)}) async-start(), calls=%async_computation.8 | async-start | bytes 1597440 | tf_op jit(solution)/shard_map/all_gather | solution.py:89
  8.7 212.6 %all-gather.15.cloned.1.call-start = ((), (), s32[]{:S(2)}) async-start(), calls=%async_computation.1 | async-start | bytes 4259840 | tf_op jit(solution)/shard_map/all_gather | solution.py:131
  116.7 177.1 %all-gather.17.cloned.1.call-start = ((), (), s32[]{:S(2)}) async-start(), calls=%async_computation.2 | async-start | bytes 4259840 | tf_op jit(solution)/shard_map/all_gather | solution.py:132
  208.8 126.6 %all-reduce.27.cloned.1.call-start = ((), (), s32[]{:S(2)}) async-start(), calls=%async_computation.3 | async-start | bytes 589824 | tf_op jit(solution)/shard_map/psum | solution.py:151
  309.0 119.4 %all-gather.23.cloned.1.call-start = ((), (), s32[]{:S(2)}) async-start(), calls=%async_computation.9 | async-start | bytes 10782720 | tf_op jit(solution)/shard_map/all_gather | solution.py:90
  309.6 207.8 %all-gather.25.cloned.1.call-start = ((), (), s32[]{:S(2)}) async-start(), calls=%async_computation.10 | async-start | bytes 10782720 | tf_op jit(solution)/shard_map/all_gather | solution.py:91
  310.4 296.0 %all-gather.27.cloned.1.call-start = ((), (), s32[]{:S(2)}) async-start(), calls=%async_computation.11 | async-start | bytes 10782720 | tf_op jit(solution)/shard_map/all_gather | solution.py:92
  311.1 342.1 %all-reduce.29.cloned.1.call-start = ((), (), s32[]{:S(2)}) async-start(), calls=%async_computation.4 | async-start | bytes 589824 | tf_op jit(solution)/shard_map/psum | solution.py:162
  626.0 75.7 %all-reduce.31.cloned.1.call-start = ((), (), s32[]{:S(2)}) async-start(), calls=%async_computation.5 | async-start | bytes 589824 | tf_op jit(solution)/shard_map/psum | solution.py:176
  670.4 433.3 %reduce-scatter.12.cloned.1.call-start = ((), (), s32[]{:S(2)}) async-start(), calls=%async_computation.6 | async-start | bytes 17039360 | tf_op jit(solution)/shard_map/reduce_scatter | solution.py:205
  749.2 392.8 %all-reduce.35.cloned.1.call-start = ((), (), s32[]{:S(2)}) async-start(), calls=%async_computation.13 | async-start | bytes 851968 | tf_op jit(solution)/shard_map/psum | solution.py:214
  1105.3 836.3 %all-reduce.33.cloned.1.call-start = ((), (), s32[]{:S(2)}) async-start(), calls=%async_computation.12 | async-start | bytes 95551488
  1344.9 26.2 %collective-permute-start.30 = (f32[24,256]{1,0:T(8,128)S(1)}, f32[24,256]{1,0:T(8,128)S(1)}, u32[]{:S(2)}, u32[]{:S(2)}) collective-permute-start(f32[24,256]{1,0:T(8,128)S(1)} %get-tuple-element.148), channel_id=1, source_target_pairs={{0,30},{2,32},{4,34},{6,36},{8,38},{10,40},{12,42},{14,44},{16,46}... | collective-permute-start | bytes 73736
  1346.2 33.2 %collective-permute-start.29 = (f32[24,256]{1,0:T(8,128)S(1)}, f32[24,256]{1,0:T(8,128)S(1)}, u32[]{:S(2)}, u32[]{:S(2)}) collective-permute-start(f32[24,256]{1,0:T(8,128)S(1)} %get-tuple-element.148), channel_id=1, source_target_pairs={{0,28},{2,30},{4,32},{6,34},{8,36},{10,38},{12,40},{14,42},{16,44}... | collective-permute-start | bytes 73736
  1348.2 17.1 collective-permute-start.31
  1364.0 16.7 collective-permute-start.28
  1371.0 16.9 collective-permute-start.25
  1380.6 20.6 %collective-permute-start.23 = (f32[24,256]{1,0:T(8,128)S(1)}, f32[24,256]{1,0:T(8,128)S(1)}, u32[]{:S(2)}, u32[]{:S(2)}) collective-permute-start(f32[24,256]{1,0:T(8,128)S(1)} %get-tuple-element.148), channel_id=1, source_target_pairs={{0,16},{2,18},{4,20},{6,22},{8,24},{10,26},{12,28},{14,30},{16,32}... | collective-permute-start | bytes 73736
  1381.9 23.8 %collective-permute-start.22 = (f32[24,256]{1,0:T(8,128)S(1)}, f32[24,256]{1,0:T(8,128)S(1)}, u32[]{:S(2)}, u32[]{:S(2)}) collective-permute-start(f32[24,256]{1,0:T(8,128)S(1)} %get-tuple-element.148), channel_id=1, source_target_pairs={{0,14},{2,16},{4,18},{6,20},{8,22},{10,24},{12,26},{14,28},{16,30}... | collective-permute-start | bytes 73736
  1384.2 23.6 %collective-permute-start.21 = (f32[24,256]{1,0:T(8,128)S(1)}, f32[24,256]{1,0:T(8,128)S(1)}, u32[]{:S(2)}, u32[]{:S(2)}) collective-permute-start(f32[24,256]{1,0:T(8,128)S(1)} %get-tuple-element.148), channel_id=1, source_target_pairs={{0,12},{2,14},{4,16},{6,18},{8,20},{10,22},{12,24},{14,26},{16,28}... | collective-permute-start | bytes 73736
  1387.9 21.8 %collective-permute-start.20 = (f32[24,256]{1,0:T(8,128)S(1)}, f32[24,256]{1,0:T(8,128)S(1)}, u32[]{:S(2)}, u32[]{:S(2)}) collective-permute-start(f32[24,256]{1,0:T(8,128)S(1)} %get-tuple-element.148), channel_id=1, source_target_pairs={{0,10},{2,12},{4,14},{6,16},{8,18},{10,20},{12,22},{14,24},{16,26}... | collective-permute-start | bytes 73736
  1390.5 24.4 %collective-permute-start.19 = (f32[24,256]{1,0:T(8,128)S(1)}, f32[24,256]{1,0:T(8,128)S(1)}, u32[]{:S(2)}, u32[]{:S(2)}) collective-permute-start(f32[24,256]{1,0:T(8,128)S(1)} %get-tuple-element.148), channel_id=1, source_target_pairs={{0,8},{2,10},{4,12},{6,14},{8,16},{10,18},{12,20},{14,22},{16,24},... | collective-permute-start | bytes 73736
  1401.3 17.3 collective-permute-start.18
  1405.7 18.0 collective-permute-start.17
  1407.7 18.0 collective-permute-start.16
  1409.7 20.6 %collective-permute-start.46 = (f32[24,256]{1,0:T(8,128)S(1)}, f32[24,256]{1,0:T(8,128)S(1)}, u32[]{:S(2)}, u32[]{:S(2)}) collective-permute-start(f32[24,256]{1,0:T(8,128)S(1)} %get-tuple-element.149), channel_id=1, source_target_pairs={{0,30},{2,32},{4,34},{6,36},{8,38},{10,40},{12,42},{14,44},{16,46}... | collective-permute-start | bytes 73736
  1414.8 16.8 collective-permute-start.45
  1456.9 17.1 collective-permute-start.63
  1459.8 17.4 collective-permute-start.14
  1474.0 18.3 collective-permute-start.10
  1477.2 334.7 %collective-permute-start.9 = (f32[24,512]{1,0:T(8,128)S(1)}, f32[24,512]{1,0:T(8,128)S(1)}, u32[]{:S(2)}, u32[]{:S(2)}) collective-permute-start(f32[24,512]{1,0:T(8,128)S(1)} %get-tuple-element.147), channel_id=1, source_target_pairs={{0,20},{2,22},{4,24},{6,26},{8,28},{10,30},{12,32},{14,34},{16,36}... | collective-permute-start | bytes 147464
  1478.7 334.4 %collective-permute-start.8 = (f32[24,512]{1,0:T(8,128)S(1)}, f32[24,512]{1,0:T(8,128)S(1)}, u32[]{:S(2)}, u32[]{:S(2)}) collective-permute-start(f32[24,512]{1,0:T(8,128)S(1)} %get-tuple-element.147), channel_id=1, source_target_pairs={{0,18},{2,20},{4,22},{6,24},{8,26},{10,28},{12,30},{14,32},{16,34}... | collective-permute-start | bytes 147464
  1481.5 333.0 %collective-permute-start.7 = (f32[24,512]{1,0:T(8,128)S(1)}, f32[24,512]{1,0:T(8,128)S(1)}, u32[]{:S(2)}, u32[]{:S(2)}) collective-permute-start(f32[24,512]{1,0:T(8,128)S(1)} %get-tuple-element.147), channel_id=1, source_target_pairs={{0,16},{2,18},{4,20},{6,22},{8,24},{10,26},{12,28},{14,30},{16,32}... | collective-permute-start | bytes 147464
  1483.1 332.6 %collective-permute-start.6 = (f32[24,512]{1,0:T(8,128)S(1)}, f32[24,512]{1,0:T(8,128)S(1)}, u32[]{:S(2)}, u32[]{:S(2)}) collective-permute-start(f32[24,512]{1,0:T(8,128)S(1)} %get-tuple-element.147), channel_id=1, source_target_pairs={{0,14},{2,16},{4,18},{6,20},{8,22},{10,24},{12,26},{14,28},{16,30}... | collective-permute-start | bytes 147464
  1492.3 324.7 %collective-permute-start.5 = (f32[24,512]{1,0:T(8,128)S(1)}, f32[24,512]{1,0:T(8,128)S(1)}, u32[]{:S(2)}, u32[]{:S(2)}) collective-permute-start(f32[24,512]{1,0:T(8,128)S(1)} %get-tuple-element.147), channel_id=1, source_target_pairs={{0,12},{2,14},{4,16},{6,18},{8,20},{10,22},{12,24},{14,26},{16,28}... | collective-permute-start | bytes 147464
  1813.1 22.9 %collective-permute-start.3 = (f32[24,512]{1,0:T(8,128)S(1)}, f32[24,512]{1,0:T(8,128)S(1)}, u32[]{:S(2)}, u32[]{:S(2)}) collective-permute-start(f32[24,512]{1,0:T(8,128)S(1)} %get-tuple-element.147), channel_id=1, source_target_pairs={{0,8},{2,10},{4,12},{6,14},{8,16},{10,18},{12,20},{14,22},{16,24},... | collective-permute-start | bytes 147464
  1814.5 26.8 %collective-permute-start.2 = (f32[24,512]{1,0:T(8,128)S(1)}, f32[24,512]{1,0:T(8,128)S(1)}, u32[]{:S(2)}, u32[]{:S(2)}) collective-permute-start(f32[24,512]{1,0:T(8,128)S(1)} %get-tuple-element.147), channel_id=1, source_target_pairs={{0,6},{2,8},{4,10},{6,12},{8,14},{10,16},{12,18},{14,20},{16,22},{... | collective-permute-start | bytes 147464
  1815.8 28.8 %collective-permute-start.1 = (f32[24,512]{1,0:T(8,128)S(1)}, f32[24,512]{1,0:T(8,128)S(1)}, u32[]{:S(2)}, u32[]{:S(2)}) collective-permute-start(f32[24,512]{1,0:T(8,128)S(1)} %get-tuple-element.147), channel_id=1, source_target_pairs={{0,4},{2,6},{4,8},{6,10},{8,12},{10,14},{12,16},{14,18},{16,20},{1... | collective-permute-start | bytes 147464
  1817.1 30.4 %collective-permute-start = (f32[24,512]{1,0:T(8,128)S(1)}, f32[24,512]{1,0:T(8,128)S(1)}, u32[]{:S(2)}, u32[]{:S(2)}) collective-permute-start(f32[24,512]{1,0:T(8,128)S(1)} %get-tuple-element.147), channel_id=1, source_target_pairs={{0,2},{2,4},{4,6},{6,8},{8,10},{10,12},{12,14},{14,16},{16,18},{18... | collective-permute-start | bytes 147464
  1821.9 34.6 %collective-permute-start.62 = (f32[512,24]{0,1:T(8,128)S(1)}, f32[512,24]{0,1:T(8,128)S(1)}, u32[]{:S(2)}, u32[]{:S(2)}) collective-permute-start(f32[512,24]{0,1:T(8,128)S(1)} %get-tuple-element.150), channel_id=1, source_target_pairs={{0,30},{2,32},{4,34},{6,36},{8,38},{10,40},{12,42},{14,44},{16,46}... | collective-permute-start | bytes 147464
  1836.1 21.9 %collective-permute-start.61 = (f32[512,24]{0,1:T(8,128)S(1)}, f32[512,24]{0,1:T(8,128)S(1)}, u32[]{:S(2)}, u32[]{:S(2)}) collective-permute-start(f32[512,24]{0,1:T(8,128)S(1)} %get-tuple-element.150), channel_id=1, source_target_pairs={{0,28},{2,30},{4,32},{6,34},{8,36},{10,38},{12,40},{14,42},{16,44}... | collective-permute-start | bytes 147464
  1841.2 18.0 collective-permute-start.60
  1858.0 28.2 %collective-permute-start.56 = (f32[512,24]{0,1:T(8,128)S(1)}, f32[512,24]{0,1:T(8,128)S(1)}, u32[]{:S(2)}, u32[]{:S(2)}) collective-permute-start(f32[512,24]{0,1:T(8,128)S(1)} %get-tuple-element.150), channel_id=1, source_target_pairs={{0,18},{2,20},{4,22},{6,24},{8,26},{10,28},{12,30},{14,32},{16,34}... | collective-permute-start | bytes 147464
  1859.3 30.6 %collective-permute-start.55 = (f32[512,24]{0,1:T(8,128)S(1)}, f32[512,24]{0,1:T(8,128)S(1)}, u32[]{:S(2)}, u32[]{:S(2)}) collective-permute-start(f32[512,24]{0,1:T(8,128)S(1)} %get-tuple-element.150), channel_id=1, source_target_pairs={{0,16},{2,18},{4,20},{6,22},{8,24},{10,26},{12,28},{14,30},{16,32}... | collective-permute-start | bytes 147464
  1860.6 32.7 %collective-permute-start.54 = (f32[512,24]{0,1:T(8,128)S(1)}, f32[512,24]{0,1:T(8,128)S(1)}, u32[]{:S(2)}, u32[]{:S(2)}) collective-permute-start(f32[512,24]{0,1:T(8,128)S(1)} %get-tuple-element.150), channel_id=1, source_target_pairs={{0,14},{2,16},{4,18},{6,20},{8,22},{10,24},{12,26},{14,28},{16,30}... | collective-permute-start | bytes 147464
  1864.0 31.5 %collective-permute-start.53 = (f32[512,24]{0,1:T(8,128)S(1)}, f32[512,24]{0,1:T(8,128)S(1)}, u32[]{:S(2)}, u32[]{:S(2)}) collective-permute-start(f32[512,24]{0,1:T(8,128)S(1)} %get-tuple-element.150), channel_id=1, source_target_pairs={{0,12},{2,14},{4,16},{6,18},{8,20},{10,22},{12,24},{14,26},{16,28}... | collective-permute-start | bytes 147464
  1870.2 30.6 %collective-permute-start.52 = (f32[512,24]{0,1:T(8,128)S(1)}, f32[512,24]{0,1:T(8,128)S(1)}, u32[]{:S(2)}, u32[]{:S(2)}) collective-permute-start(f32[512,24]{0,1:T(8,128)S(1)} %get-tuple-element.150), channel_id=1, source_target_pairs={{0,10},{2,12},{4,14},{6,16},{8,18},{10,20},{12,22},{14,24},{16,26}... | collective-permute-start | bytes 147464
  (100 other events, 5654.3 us)
Sparse Core Ops, SparseCore 0:
  11.3 70.4 all-gather.18
  85.1 63.5 all-gather.20
  152.4 68.8 all-gather.14
  224.9 68.8 all-gather.16
  309.2 26.1 all-reduce.26
  338.4 90.0 all-gather.22
  431.5 85.8 all-gather.24
  520.5 85.8 all-gather.26
  626.2 27.0 all-reduce.28
  670.5 31.2 all-reduce.30
  749.3 354.3 reduce-scatter.11
  1106.6 35.2 all-reduce.34
  1144.7 796.8 all-reduce.32
where the time goes:
time: 1970 us; the launch traced here: 1950 us
  waiting for transfers between devices  794 us (40%)
  blocking collectives  709 us (36%)
  starting transfers between devices  216 us (11%)
  local copies, waits for them, and re-layouts  89.5 us (5%)
  matrix products  84.7 us (4%)
  other arithmetic  38.3 us (2%)
    unnamed x2, blocking collectives  513 us
    reduce_scatter x1, waiting for transfers between devices, shards(): lax.psum_scatter(folded[1], 'ctx', scatter_dimension=0, tiled=True)  335 us
    unnamed x65, starting transfers between devices  215 us
    all_gather x1, blocking collectives, shards(): lax.all_gather(w_key, 'ctx', axis=0, tiled=True)  101 us
    all_gather x1, blocking collectives, shards(): lax.all_gather(w_value, 'ctx', axis=0, tiled=True)  90.9 us
    all_gather x1, waiting for transfers between devices, shards(): lax.all_gather(w_gate, 'ctx', axis=0, tiled=True)  90.5 us
    all_gather x1, waiting for transfers between devices, shards(): lax.all_gather(w_up, 'ctx', axis=0, tiled=True)  75.8 us
    all_gather x1, waiting for transfers between devices, shards(): values = lax.all_gather(value_low, 'ctx', axis=0, tiled=True)  72.5 us
  transfers between devices with their start and end apart: 77, of which 12 were waited for; matrix products, arithmetic and copies ran while one was open for 16% of the time, Pallas kernels for 0%

commit v1 on v0

v1 whole, which is shorter than its diff:
```python
import math

import jax
import jax.numpy as jnp
from jax import lax
from jax.sharding import Mesh, PartitionSpec as P

HD = 256
EPS = 1e-06
THETA = 1000000.0
BF = jnp.bfloat16
F32 = jnp.float32
CTX = ("y", "z", "x", "c")


def matmul(left, right):
    return jnp.dot(left, right, preferred_element_type=F32)


def inner_rows(left, right):
    return lax.dot_general(left, right, (((0,), (0,)), ((), ())), preferred_element_type=F32)


def inner_cols(left, right):
    return lax.dot_general(left, right, (((1,), (1,)), ((), ())), preferred_element_type=F32)


def rms_scale(values, gain):
    return values * lax.rsqrt(jnp.mean(values * values, axis=-1, keepdims=True) + EPS) * gain


def rotate(values, cosine_table, sine_table):
    half_width = values.shape[-1] // 2
    first = values[..., :half_width]
    second = values[..., half_width:]
    return jnp.concatenate(
        [first * cosine_table - second * sine_table, second * cosine_table + first * sine_table],
        axis=-1,
    )


def geglu(gate_pre, up_pre):
    return jax.nn.gelu(gate_pre, approximate=True) * up_pre


def tables(positions, head_width):
    frequency = jnp.arange(head_width // 2, dtype=F32)
    inverse = jnp.exp(frequency * (-2.0 * math.log(THETA) / head_width))
    angles = positions.astype(F32)[:, None] * inverse[None, :]
    return (jnp.cos(angles), jnp.sin(angles))


def shift(values, axis, step=1):
    size = lax.axis_size(axis)
    return lax.ppermute(values, axis, [(i, (i + step) % size) for i in range(size)])


def gather_ring(block, axis):
    half = block.shape[0] // 2
    previous = shift(block, axis, 1)
    following = shift(block, axis, -1)
    far_low = shift(previous[:half], axis, 1)
    far_high = shift(following[half:], axis, -1)
    return [block, following, jnp.concatenate([far_low, far_high], 0), previous]


def reduce_ring(chunks, axis):
    rows = chunks[0].shape[0]
    half = (rows // 2 + 7) // 8 * 8
    from_previous = shift(chunks[2][:half], axis, 1)
    from_next = shift(chunks[2][half:], axis, -1)
    forward = jnp.concatenate(
        [(chunks[1][:half].astype(F32) + from_previous.astype(F32)).astype(BF), chunks[1][half:]], 0
    )
    backward = jnp.concatenate(
        [chunks[3][:half], (chunks[3][half:].astype(F32) + from_next.astype(F32)).astype(BF)], 0
    )
    return (
        chunks[0].astype(F32)
        + shift(forward, axis, 1).astype(F32)
        + shift(backward, axis, -1).astype(F32)
    )


def split_rows(values, parts):
    size = values.shape[0] // parts
    return [values[i * size : (i + 1) * size] for i in range(parts)]


def pick(core, first, second):
    return jnp.where(core == 0, first, second)


def shards(
    hidden_in,
    out_grad,
    block_order,
    norm_gains,
    head_gains,
    w_query,
    w_key,
    w_value,
    w_out,
    w_gate,
    w_up,
    w_down,
):
    tokens, width = hidden_in.shape
    y, z, x, core = (lax.axis_index(name) for name in CTX)
    other = 1 - core
    piece = width // 64
    units = w_gate.shape[1] // 2
    padded = (units + 127) // 128 * 128
    quarter = width // 4

    out_t, down_t = w_out.T, w_down.T

    def units_of(which):
        cut = [
            jnp.pad(lax.dynamic_slice_in_dim(w, which * units, units, 1), ((0, 0), (0, padded - units)))
            for w in (w_gate, w_up, down_t)
        ]
        return jnp.concatenate(cut, 1)

    def heads_of(which):
        cut = [lax.dynamic_slice_in_dim(w, which * HD, HD, 1) for w in (w_query, out_t)]
        return jnp.concatenate(cut + [w_key, w_value], 1)

    def chip_rows(of):
        mine, got = of(core), shift(of(other), "c")
        rows = pick(core, jnp.concatenate([mine, got], 0), jnp.concatenate([got, mine], 0))
        return jnp.concatenate([rows, shift(rows, "y")], 0)

    head_rows = chip_rows(heads_of)
    ffn_rows = chip_rows(units_of)
    ffn_w = lax.all_gather(ffn_rows, ("z", "x"), axis=0, tiled=True)
    head_z = jnp.concatenate(gather_ring(head_rows, "z"), 0)
    head_w = jnp.concatenate(gather_ring(head_z, "x"), 0)
    gate_up_w, down_w = ffn_w[:, : 2 * padded], ffn_w[:, 2 * padded :]
    query_w, out_w = head_w[:, :HD], head_w[:, HD : 2 * HD]
    key_w, value_w, pair_w = head_w[:, 2 * HD : 3 * HD], head_w[:, 3 * HD :], head_w[:, 2 * HD :]

    place = jnp.arange(width, dtype=jnp.int32)
    major, second = place // quarter, place // (quarter // 4) % 4
    tail_y, tail = place // (2 * piece) % 2, place % (2 * piece)

    def natural(z_at, x_at):
        return ((y + tail_y) % 2) * (width // 2) + z_at * (8 * piece) + x_at * (2 * piece) + tail

    by_gather = natural(major, second)
    by_x = natural((z + second) % 4, (x + major) % 4)
    by_z = natural((z + major) % 4, (x + second) % 4)

    def order(source, target):
        return (source[:, None] == target[None, :]).astype(BF)

    to_gather, to_x = order(place, by_gather), order(place, by_x)
    from_gather, from_x = order(by_gather, place), order(by_x, place)

    def reorder(values, moves):
        return matmul(values, moves).astype(BF)

    def both_cores(values):
        return jnp.concatenate([values, shift(values, "c")], 0)

    def sum_parts(partial, moves):
        low = reorder(partial.astype(BF), moves)
        chip = (low[:tokens].astype(F32) + shift(low[tokens:], "c").astype(F32)).astype(BF)
        return chip.astype(F32) + shift(chip, "s").astype(F32)

    offsets = jnp.arange(tokens, dtype=jnp.int32)

    def positions_of(places):
        return (block_order[places.reshape(-1)][:, None] * tokens + offsets[None, :]).reshape(-1)

    def device_of(y_at, z_at, x_at, core_at):
        return y_at * 32 + z_at * 8 + x_at * 2 + core_at

    steps = jnp.arange(4, dtype=jnp.int32)
    ring = device_of(
        (y + steps[None, None, :2]) % 2, (z + steps[None, :, None]) % 4, (x + steps[:, None, None]) % 4, 0
    )
    key_pos = [positions_of(ring + core), positions_of(ring + other)]
    own_pos = positions_of(device_of(y, z, x, core))
    chip_pos = jnp.concatenate([own_pos, positions_of(device_of(y, z, x, other))])
    cosine_table, sine_table = tables(chip_pos, HD)

    attn_val, pre_attn_back = jax.vjp(rms_scale, hidden_in, norm_gains[0])
    attn_x = reorder(attn_val.astype(BF), to_x)
    attn_chip = both_cores(attn_x)
    key_pre = matmul(attn_x, key_w)
    value_low = matmul(attn_x, value_w).astype(BF)
    key_val, key_back = jax.vjp(
        lambda values, gain: rotate(rms_scale(values, gain), cosine_table[:tokens], sine_table[:tokens]),
        key_pre,
        head_gains[1],
    )
    key_low = key_val.astype(BF)
    pair_low = jnp.concatenate([key_low, value_low], 1)
    pair_rows = jnp.concatenate([pair_low, shift(pair_low, "y")], 0)
    key_z = jnp.concatenate(gather_ring(pair_rows[:, :HD], "z"), 0)
    keys = jnp.concatenate(gather_ring(key_z, "x"), 0)
    value_x = jnp.concatenate(gather_ring(pair_rows[:, HD:], "x"), 0)
    value_parts = [split_rows(part, 4) for part in gather_ring(value_x, "z")]
    values = jnp.concatenate([value_parts[j][i] for i in range(4) for j in range(4)], 0)
    all_keys = [keys, shift(keys, "c")]
    all_values = [values, shift(values, "c")]

    query_pre = matmul(attn_chip, query_w)
    query_val, query_back = jax.vjp(
        lambda values, gain: rotate(rms_scale(values, gain), cosine_table, sine_table),
        query_pre,
        head_gains[0],
    )
    score_scale = HD ** (-0.5)
    queries = (query_val.astype(BF).astype(F32) * score_scale).astype(BF)
    weights, total, accum = [], 0.0, 0.0
    for part in range(2):
        scores = inner_cols(queries, all_keys[part])
        allowed = chip_pos[:, None] >= key_pos[part][None, :]
        weight = jnp.where(allowed, jnp.exp(scores), 0.0)
        total = total + jnp.sum(weight, axis=1)
        weights.append(weight.astype(BF))
        accum = accum + matmul(weights[part], all_values[part])
    inverse_total = (1.0 / total)[:, None]
    attn_rows = accum * inverse_total
    mixed_low = attn_rows.astype(BF)
    attn_out = sum_parts(inner_cols(mixed_low, out_w), from_x)
    post_attn, post_attn_back = jax.vjp(rms_scale, attn_out, norm_gains[1])
    mid_state = hidden_in + post_attn

    ffn_val, ffn_norm_back = jax.vjp(rms_scale, mid_state, norm_gains[2])
    ffn_chip = both_cores(reorder(ffn_val.astype(BF), to_gather))
    gate_up = matmul(ffn_chip, gate_up_w)
    hidden_val, geglu_back = jax.vjp(geglu, gate_up[:, :padded], gate_up[:, padded:])
    hidden_low = hidden_val.astype(BF)
    ffn_out = sum_parts(inner_cols(hidden_low, down_w), from_gather)
    post_ffn, post_ffn_back = jax.vjp(rms_scale, ffn_out, norm_gains[3])
    block_out = mid_state + post_ffn

    ffn_grad, gain_four = post_ffn_back(out_grad)
    ffn_grad_chip = both_cores(reorder(ffn_grad.astype(BF), to_gather))
    gate_grad, up_grad = geglu_back(matmul(ffn_grad_chip, down_w))
    gate_up_low = jnp.concatenate([gate_grad.astype(BF), up_grad.astype(BF)], 1)
    ffn_norm_grad = sum_parts(inner_cols(gate_up_low, gate_up_w), from_gather)
    mid_from, gain_three = ffn_norm_back(ffn_norm_grad)
    mid_grad = out_grad + mid_from

    half = padded // 2
    sources = jnp.concatenate([ffn_chip, ffn_grad_chip], 0)
    none_wide, none_half = jnp.zeros((2 * tokens, padded), BF), jnp.zeros((2 * tokens, half), BF)

    def ffn_chunks(first, second, target):
        grads = jnp.concatenate(
            [jnp.concatenate([first, none_half], 1), jnp.concatenate([none_wide, second], 1)], 0
        )
        chunks = {}
        for k in (2, 1, 3, 0):
            rows = reorder(sources, order(by_gather, target[k * quarter : (k + 1) * quarter]))
            chunks[k] = inner_rows(rows, grads).astype(BF)
        return [chunks[k] for k in range(4)]

    def reduce_two(chunks, first, second):
        low = reduce_ring(chunks, first).astype(BF)
        return reduce_ring(split_rows(low, 4), second)

    def reduce_y(values):
        low = values.astype(BF)
        own, far = split_rows(low, 2)
        return own.astype(F32) + shift(far, "y").astype(F32)

    def swap_cores(rows):
        low = rows.astype(BF)
        first, second = split_rows(low, 2)
        return pick(core, first, second).astype(F32), shift(pick(core, second, first), "c").astype(F32)

    ffn_first = reduce_two(ffn_chunks(gate_up_low[:, :padded], hidden_low[:, :half], by_x), "x", "z")
    ffn_second = reduce_two(ffn_chunks(gate_up_low[:, padded:], hidden_low[:, half:], by_z), "z", "x")
    ffn_mine, ffn_got = swap_cores(reduce_y(jnp.concatenate([ffn_first, ffn_second], 1)))

    def joined(start, size, mine, got):
        left, right = mine[:, start : start + size], got[:, start : start + size]
        return pick(core, jnp.concatenate([left, right], 1), jnp.concatenate([right, left], 1))

    gate_wgrad = joined(0, units, ffn_mine, ffn_got)
    up_wgrad = joined(padded + half, units, ffn_mine, ffn_got)

    def down_of(values):
        return jnp.concatenate([values[:, padded : padded + half], values[:, 2 * padded + half :]], 1)

    down_wgrad = joined(0, units, down_of(ffn_mine), down_of(ffn_got)).T

    attn_grad, gain_two = post_attn_back(mid_grad)
    attn_grad_chip = both_cores(reorder(attn_grad.astype(BF), to_x))
    rows_grad = matmul(attn_grad_chip, out_w).astype(BF)
    rows_wide = rows_grad.astype(F32)
    row_dot = jnp.sum(rows_wide * attn_rows, axis=1)[:, None]
    rows_scaled = (rows_wide * inverse_total).astype(BF)
    query_grad, key_parts, value_parts = 0.0, {}, {}
    for part in (1, 0):
        prob_grad = inner_cols(rows_grad, all_values[part])
        score_grad = (weights[part].astype(F32) * ((prob_grad - row_dot) * inverse_total)).astype(BF)
        query_grad = query_grad + matmul(score_grad, all_keys[part])
        key_parts[part] = inner_rows(score_grad, queries).astype(BF)
        value_parts[part] = inner_rows(weights[part], rows_scaled).astype(BF)
    key_sum = (key_parts[0].astype(F32) + shift(key_parts[1], "c").astype(F32)).astype(BF)
    value_sum = (value_parts[0].astype(F32) + shift(value_parts[1], "c").astype(F32)).astype(BF)
    key_own = reduce_two(split_rows(key_sum, 4), "x", "z")
    value_grid = value_sum.reshape(4, 4, 2 * tokens, HD)
    value_own = reduce_two([value_grid[:, k].reshape(-1, HD) for k in range(4)], "z", "x")
    pair_low = reduce_y(jnp.concatenate([key_own, value_own], 1)).astype(BF)
    pair_grad = pair_low.astype(F32) + shift(pair_low, "s").astype(F32)

    query_pre_grad, query_gain = query_back(query_grad * score_scale)
    query_gain = query_gain + shift(query_gain, "s")
    query_pre_low = query_pre_grad.astype(BF)
    attn_norm_sum = sum_parts(inner_cols(query_pre_low, query_w), from_x)
    key_pre_grad, key_gain = key_back(pair_grad[:, :HD])
    key_pre_low = key_pre_grad.astype(BF)
    value_grad_low = pair_grad[:, HD:].astype(BF)
    pair_part = inner_cols(jnp.concatenate([key_pre_low, value_grad_low], 1), pair_w).astype(BF)
    attn_norm_grad = attn_norm_sum + reorder(pair_part, from_x).astype(F32)
    input_from, gain_one = pre_attn_back(attn_norm_grad)
    input_grad = mid_grad + input_from

    kept, sent = pick(core, key_pre_low, value_grad_low), pick(core, value_grad_low, key_pre_low)
    pair_chip = jnp.concatenate([kept, shift(sent, "c")], 0)
    heads = [
        jnp.pad(gain.reshape(64, HD // 64), ((0, 0), (0, piece - HD // 64))).reshape(width)
        for gain in (query_gain, key_gain)
    ]
    gains = jnp.stack([gain_one, gain_two, gain_three, gain_four] + heads, 1)
    gains = jnp.pad(gains, ((0, 0), (0, 128 - gains.shape[1]))).astype(BF)
    head_grads_all = jnp.concatenate(
        [
            inner_rows(attn_chip, query_pre_low),
            inner_rows(attn_grad_chip, mixed_low),
            inner_rows(attn_chip, pair_chip),
            inner_rows(to_x, gains),
        ],
        1,
    ).astype(BF)
    head_own = reduce_two(split_rows(head_grads_all, 4), "x", "z")
    head_mine, head_got = swap_cores(reduce_y(head_own))
    query_wgrad = joined(0, HD, head_mine, head_got)
    out_wgrad = joined(HD, HD, head_mine, head_got).T
    pair_wgrad = joined(2 * HD, HD, head_mine, head_got)
    gain_sums = head_mine[:, 3 * HD :] + head_got[:, 3 * HD :]
    return (
        block_out,
        input_grad,
        query_wgrad,
        pair_wgrad[:, :HD],
        pair_wgrad[:, HD:],
        out_wgrad,
        gate_wgrad,
        up_wgrad,
        down_wgrad,
        gain_sums[:, :4].T,
        gain_sums[: HD // 64, 4:6].T,
    )


def solution(mesh):
    fine = Mesh(mesh.devices.reshape(2, 4, 4, 2, 2), ("y", "z", "x", "c", "s"))
    placed = (
        P(CTX, None),
        P(CTX, None),
        P(),
        P(),
        P(),
        P(CTX, "s"),
        P(CTX, None),
        P(CTX, None),
        P("s", CTX),
        P(CTX, "s"),
        P(CTX, "s"),
        P("s", CTX),
    )
    return jax.shard_map(
        shards,
        mesh=fine,
        in_specs=placed,
        out_specs=(
            P(CTX, None),
            P(CTX, None),
            P(CTX, "s"),
            P(CTX, None),
            P(CTX, None),
            P("s", CTX),
            P(CTX, "s"),
            P(CTX, "s"),
            P("s", CTX),
            P(None, CTX),
            P(None, CTX),
        ),
        check_vma=False,
    )
```

time: 1970 us -> 624 us (0.32)
  blocking collectives: 709 us -> 0 us
  waiting for transfers between devices: 794 us -> 173 us
  starting transfers between devices: 216 us -> 139 us
  matrix products: 84.7 us -> 122 us
  other arithmetic: 38.3 us -> 59.9 us
    unnamed x2 -> x0, blocking collectives: 513 us -> none
    reduce_scatter x1 -> x0, waiting for transfers between devices: 335 us -> none  [shards(): lax.psum_scatter(folded[1], 'ctx', scatter_dimension=0, tiled=True)]
    all_gather x7 -> x1, waiting for transfers between devices: 309 us -> 0.01 us  [shards(): ffn_w = lax.all_gather(ffn_rows, ('z', 'x'), axis=0, tiled=True)]
    unnamed x65 -> x0, starting transfers between devices: 215 us -> none
    all_gather x2 -> x0, blocking collectives: 192 us -> none  [the longest x1 101 us: shards(): lax.all_gather(w_key, 'ctx', axis=0, tiled=True)]
    ppermute x0 -> x93, waiting for transfers between devices: none -> 173 us  [shift(): lax.ppermute(values, axis, [(i, (i + step) % size) for i in range(size)])]
    ppermute x0 -> x93, starting transfers between devices: none -> 139 us  [shift(): lax.ppermute(values, axis, [(i, (i + step) % size) for i in range(size)])]
    psum x4 -> x0, waiting for transfers between devices: 106 us -> none  [the longest x1 31.4 us: shards(): lax.psum((inner_cols(gate_low, gate_full) + inner_cols(up_low, up_full))....]
  transfers between devices with their start and end apart: 77 -> 94, of which waited for: 12 -> 40; matrix products, arithmetic and copies ran while one was open for 16% -> 37% of each run, Pallas kernels for 0% -> 0%
where the time goes in v1:
time: 624 us; the launch traced here: 612 us
  waiting for transfers between devices  173 us (28%)
  starting transfers between devices  139 us (22%)
  matrix products  122 us (20%)
  local copies, waits for them, and re-layouts  99.7 us (16%)
  other arithmetic  59.9 us (10%)
  between operations  18.3 us (3%)
    ppermute x93, waiting for transfers between devices, shift(): lax.ppermute(values, axis, [(i, (i + step) % size) for i in range(size)])  173 us
    ppermute x93, starting transfers between devices, shift(): lax.ppermute(values, axis, [(i, (i + step) % size) for i in range(size)])  139 us
    dot_general x19, matrix products, matmul(): return jnp.dot(left, right, preferred_element_type=F32)  56.9 us
    dot_general x16, matrix products, inner_rows(): lax.dot_general(left, right, (((0,), (0,)), ((), ())), preferred_element_...  52.6 us
    unnamed x299, local copies, waits for them, and re-layouts  37.9 us
    dot_general x4, matrix products, inner_cols(): lax.dot_general(left, right, (((1,), (1,)), ((), ())), preferred_element_...  12.6 us
  transfers between devices with their start and end apart: 94, of which 40 were waited for; matrix products, arithmetic and copies ran while one was open for 37% of the time, Pallas kernels for 0%

profile of v1, /device:TPU:1, one launch (start us, length us, event | category | flops | bytes accessed | tf_op | source)
XLA Modules:
  0.0 612.4 jit_solution(8770895978738714284)
XLA Ops:
  12.5 3.1 collective-permute-start.34
  15.5 9.7 %collective-permute-done.34 = bf16[36,5376]{1,0:T(8,128)(2,1)S(1)} collective-permute-done((bf16[36,5376]{1,0:T(8,128)(2,1)S(1)}, bf16[36,5376]{1,0:T(8,128)(2,1)S(1)}, u32[]{:S(2)}, u32[]{:S(2)}) %collective-permute-start.34) | collective-permute-done | bytes 387104 | tf_op jit(solution)/shard_map/ppermute | solution.py:55
  28.5 3.1 collective-permute-start.2
  43.6 3.7 collective-permute-done.5
  53.0 3.0 collective-permute-start
  58.6 9.1 %collective-permute-done.7 = bf16[288,1024]{1,0:T(8,128)(2,1)S(1)} collective-permute-done((bf16[288,1024]{1,0:T(8,128)(2,1)S(1)}, bf16[288,1024]{1,0:T(8,128)(2,1)S(1)}, u32[]{:S(2)}, u32[]{:S(2)}) %collective-permute-start.7) | collective-permute-done | bytes 589856 | tf_op jit(solution)/shard_map/ppermute | solution.py:55
  71.7 11.1 %collective-permute-done.10 = bf16[144,1024]{1,0:T(8,128)(2,1)S(1)} collective-permute-done((bf16[144,1024]{1,0:T(8,128)(2,1)S(1)}, bf16[144,1024]{1,0:T(8,128)(2,1)S(1)}, u32[]{:S(2)}, u32[]{:S(2)}) %collective-permute-start.10) | collective-permute-done | bytes 294944 | tf_op jit(solution)/shard_map/ppermute | solution.py:55
  86.4 12.2 %concatenate.239 = bf16[1152,1024]{1,0:T(8,128)(2,1)S(1)} concatenate(bf16[36,1024]{1,0:T(8,128)(2,1)} %copy-done.34, bf16[36,1024]{1,0:T(8,128)(2,1)} %copy-done.48, bf16[72,1024]{1,0:T(8,128)(2,1)} %copy-done.43, bf16[36,1024]{1,0:T(8,128)(2,1)} %copy-done.66, bf16[36,1024]{1,0:T(8,128)(2,1)} %copy-done.67, bf16[72,1024]{1,0:T(8,128)(2,1)} %copy-done.42, ...), dimensions={0} | concatenate | bytes 4718592 | tf_op jit(solution)/shard_map/concatenate | solution.py:138
  109.4 2.9 collective-permute-done.11
  116.1 6.0 collective-permute-done.13
  137.1 3.7 collective-permute-done.17
  153.2 10.7 %collective-permute-start.28 = (bf16[4096,256]{1,0:T(8,128)(2,1)S(1)}, bf16[4096,256]{1,0:T(8,128)(2,1)}, u32[]{:S(2)}, u32[]{:S(2)}) collective-permute-start(bf16[4096,256]{1,0:T(8,128)(2,1)S(1)} %constant_dynamic-update-slice_fusion.5), channel_id=1, source_target_pairs={{0,2},{2,0},{1,3},{3,1},{4,6},{6,4},{5,7},{7,5},{8,10},{10,8},{9,1... | collective-permute-start | bytes 6291464 | tf_op jit(solution)/shard_map/ppermute | solution.py:55
  179.9 3.7 fusion.351
  188.8 3.5 fusion.47
  197.3 7.4 %collective-permute-done.31 = bf16[128,1152]{1,0:T(8,128)(2,1)S(1)} collective-permute-done((bf16[128,1152]{1,0:T(8,128)(2,1)S(1)}, bf16[128,1152]{1,0:T(8,128)(2,1)S(1)}, u32[]{:S(2)}, u32[]{:S(2)}) %collective-permute-start.31) | collective-permute-done | bytes 294944 | tf_op jit(solution)/shard_map/ppermute | solution.py:55
  209.9 6.1 fusion.2
  219.4 5.8 fusion.49
  231.4 5.9 collective-permute-done.36
  243.7 5.8 fusion.67
  249.4 8.9 %fusion.50 = bf16[256,1152]{1,0:T(8,128)(2,1)} fusion(s32[1152]{0:T(1024)} %copy-done.104, bf16[1152,5376]{1,0:T(8,128)(2,1)} %all-gather.2.cloned.1.call-done, bf16[256,1792]{1,0:T(8,128)(2,1)} %get-tuple-element.78, bf16[256,1792]{1,0:T(8,128)(2,1)} %get-tuple-element.77), kind=kOutput, calls=%fused_computation.79 | convolution fusion | flops 2798993408 | bytes 10690560 | tf_op jit(solution)/shard_map/dot_general | solution.py:17
  260.1 4.7 convolution_convert_fusion.9
  267.5 4.7 convolution_convert_fusion.10
  274.9 4.7 convolution_convert_fusion.5
  285.1 4.7 convolution_convert_fusion.8
  289.9 4.8 convolution_convert_fusion.6
  294.6 4.8 convolution_convert_fusion.4
  299.4 5.3 fusion.27
  307.3 5.3 fusion.26
  339.8 3.6 multiply_convert_fusion
  371.1 3.4 add_convert_fusion.3
  374.6 25.3 %collective-permute-done.86 = bf16[288,2688]{1,0:T(8,128)(2,1)S(1)} collective-permute-done((bf16[288,2688]{1,0:T(8,128)(2,1)}, bf16[288,2688]{1,0:T(8,128)(2,1)S(1)}, u32[]{:S(2)}, u32[]{:S(2)}) %collective-permute-start.86) | collective-permute-done | bytes 1548320 | tf_op jit(solution)/shard_map/ppermute | solution.py:55
  404.1 4.6 collective-permute-done.89
  415.1 3.7 collective-permute-done.82
  421.2 3.9 collective-permute-done.80
  426.7 6.8 %collective-permute-done.88 = bf16[72,2688]{1,0:T(8,128)(2,1)S(1)} collective-permute-done((bf16[72,2688]{1,0:T(8,128)(2,1)S(1)}, bf16[72,2688]{1,0:T(8,128)(2,1)S(1)}, u32[]{:S(2)}, u32[]{:S(2)}) %collective-permute-start.88) | collective-permute-done | bytes 387104 | tf_op jit(solution)/shard_map/ppermute | solution.py:55
  477.0 6.3 %collective-permute-start.92 = (bf16[18,5376]{1,0:T(8,128)(2,1)S(1)}, bf16[18,5376]{1,0:T(8,128)(2,1)S(1)}, u32[]{:S(2)}, u32[]{:S(2)}) collective-permute-start(bf16[18,5376]{1,0:T(8,128)(2,1)S(1)} %get-tuple-element.138), channel_id=1, source_target_pairs={{0,2},{2,0},{1,3},{3,1},{4,6},{6,4},{5,7},{7,5},{8,10},{10,8},{9,1... | collective-permute-start | bytes 580616 | tf_op jit(solution)/shard_map/ppermute | solution.py:55
  484.5 3.0 collective-permute-start.56
  491.3 7.1 %collective-permute-done.56 = bf16[1024,256]{0,1:T(8,128)(2,1)S(1)} collective-permute-done((bf16[1024,256]{0,1:T(8,128)(2,1)S(1)}, bf16[1024,256]{0,1:T(8,128)(2,1)S(1)}, u32[]{:S(2)}, u32[]{:S(2)}) %collective-permute-start.56) | collective-permute-done | bytes 524320 | tf_op jit(solution)/shard_map/ppermute | solution.py:55
  510.6 5.3 collective-permute-done.61
  516.7 3.4 collective-permute-done.62
  521.2 6.8 %collective-permute-start.63 = (bf16[128,256]{0,1:T(8,128)(2,1)}, bf16[128,256]{0,1:T(8,128)(2,1)}, u32[]{:S(2)}, u32[]{:S(2)}) collective-permute-start(bf16[128,256]{0,1:T(8,128)(2,1)} %broadcast_select_fusion.2), channel_id=1, source_target_pairs={{0,2},{2,0},{1,3},{3,1},{4,6},{6,4},{5,7},{7,5},{8,10},{10,8},{9,1... | collective-permute-start | bytes 196616 | tf_op jit(solution)/shard_map/ppermute | solution.py:55
  528.0 4.0 multiply_reduce_fusion.3
  541.2 9.9 %collective-permute-done.65 = bf16[144,896]{0,1:T(8,128)(2,1)S(1)} collective-permute-done((bf16[144,896]{0,1:T(8,128)(2,1)S(1)}, bf16[144,896]{0,1:T(8,128)(2,1)S(1)}, u32[]{:S(2)}, u32[]{:S(2)}) %collective-permute-start.65) | collective-permute-done | bytes 258080 | tf_op jit(solution)/shard_map/ppermute | solution.py:55
  563.0 5.0 collective-permute-done.66
  575.2 3.1 collective-permute-done.71
  584.1 3.5 collective-permute-done.70
  589.8 4.5 collective-permute-done.73
  594.5 6.1 collective-permute-start.74
  (708 shorter events, 310.5 us)
Async XLA Ops:
  7.2 202.7 %all-gather.2.cloned.1.call-start = ((), (), s32[]{:S(2)}) async-start(), calls=%async_computation | async-start | bytes 13160448 | tf_op jit(solution)/shard_map/all_gather | solution.py:136
  12.5 12.8 %collective-permute-start.34 = (bf16[36,5376]{1,0:T(8,128)(2,1)S(1)}, bf16[36,5376]{1,0:T(8,128)(2,1)S(1)}, u32[]{:S(2)}, u32[]{:S(2)}) collective-permute-start(bf16[36,5376]{1,0:T(8,128)(2,1)S(1)} %maximum_select_fusion), channel_id=1, source_target_pairs={{0,64},{64,0},{1,65},{65,1},{2,66},{66,2},{3,67},{67,3},{4,68},{68... | collective-permute-start | bytes 1161224 | tf_op jit(solution)/shard_map/ppermute | solution.py:55
  48.0 19.7 %collective-permute-start.7 = (bf16[288,1024]{1,0:T(8,128)(2,1)S(1)}, bf16[288,1024]{1,0:T(8,128)(2,1)S(1)}, u32[]{:S(2)}, u32[]{:S(2)}) collective-permute-start(bf16[288,1024]{1,0:T(8,128)(2,1)S(1)} %concatenate.238), channel_id=1, source_target_pairs={{0,12},{4,0},{8,4},{12,8},{1,13},{5,1},{9,5},{13,9},{2,14},{6,2},{... | collective-permute-start | bytes 1769480 | tf_op jit(solution)/shard_map/ppermute | solution.py:55
  50.4 20.1 %collective-permute-start.8 = (bf16[288,1024]{1,0:T(8,128)(2,1)S(1)}, bf16[288,1024]{1,0:T(8,128)(2,1)S(1)}, u32[]{:S(2)}, u32[]{:S(2)}) collective-permute-start(bf16[288,1024]{1,0:T(8,128)(2,1)S(1)} %concatenate.238), channel_id=1, source_target_pairs={{0,4},{4,8},{8,12},{12,0},{1,5},{5,9},{9,13},{13,1},{2,6},{6,10},{... | collective-permute-start | bytes 1769480 | tf_op jit(solution)/shard_map/ppermute | solution.py:55
  53.0 47.8 %collective-permute-start = (bf16[128,1152]{1,0:T(8,128)(2,1)}, bf16[128,1152]{1,0:T(8,128)(2,1)}, u32[]{:S(2)}, u32[]{:S(2)}) collective-permute-start(bf16[128,1152]{1,0:T(8,128)(2,1)} %fusion.54), channel_id=1, source_target_pairs={{0,2},{2,0},{1,3},{3,1},{4,6},{6,4},{5,7},{7,5},{8,10},{10,8},{9,1... | collective-permute-start | bytes 884744 | tf_op jit(solution)/shard_map/ppermute | solution.py:55
  67.7 15.1 %collective-permute-start.10 = (bf16[144,1024]{1,0:T(8,128)(2,1)S(1)}, bf16[144,1024]{1,0:T(8,128)(2,1)S(1)}, u32[]{:S(2)}, u32[]{:S(2)}) collective-permute-start(bf16[144,1024]{1,0:T(8,128)(2,1)S(1)} %slice.779), channel_id=1, source_target_pairs={{0,12},{4,0},{8,4},{12,8},{1,13},{5,1},{9,5},{13,9},{2,14},{6,2},{... | collective-permute-start | bytes 884744 | tf_op jit(solution)/shard_map/ppermute | solution.py:55
  70.5 15.9 %collective-permute-start.9 = (bf16[144,1024]{1,0:T(8,128)(2,1)S(1)}, bf16[144,1024]{1,0:T(8,128)(2,1)}, u32[]{:S(2)}, u32[]{:S(2)}) collective-permute-start(bf16[144,1024]{1,0:T(8,128)(2,1)S(1)} %slice.778), channel_id=1, source_target_pairs={{0,4},{4,8},{8,12},{12,0},{1,5},{5,9},{9,13},{13,1},{2,6},{6,10},{... | collective-permute-start | bytes 884744 | tf_op jit(solution)/shard_map/ppermute | solution.py:55
  114.6 10.6 %collective-permute-start.20 = (bf16[256,256]{1,0:T(8,128)(2,1)S(1)}, bf16[256,256]{1,0:T(8,128)(2,1)S(1)}, u32[]{:S(2)}, u32[]{:S(2)}) collective-permute-start(bf16[256,256]{1,0:T(8,128)(2,1)S(1)} %get-tuple-element.149), channel_id=1, source_target_pairs={{0,12},{4,0},{8,4},{12,8},{1,13},{5,1},{9,5},{13,9},{2,14},{6,2},{... | collective-permute-start | bytes 393224 | tf_op jit(solution)/shard_map/ppermute | solution.py:55
  115.2 9.9 %collective-permute-start.21 = (bf16[256,256]{1,0:T(8,128)(2,1)S(1)}, bf16[256,256]{1,0:T(8,128)(2,1)S(1)}, u32[]{:S(2)}, u32[]{:S(2)}) collective-permute-start(bf16[256,256]{1,0:T(8,128)(2,1)S(1)} %get-tuple-element.149), channel_id=1, source_target_pairs={{0,4},{4,8},{8,12},{12,0},{1,5},{5,9},{9,13},{13,1},{2,6},{6,10},{... | collective-permute-start | bytes 393224 | tf_op jit(solution)/shard_map/ppermute | solution.py:55
  131.2 11.3 %collective-permute-start.16 = (bf16[1024,256]{1,0:T(8,128)(2,1)}, bf16[1024,256]{1,0:T(8,128)(2,1)}, u32[]{:S(2)}, u32[]{:S(2)}) collective-permute-start(bf16[1024,256]{1,0:T(8,128)(2,1)} %get-tuple-element.166), channel_id=1, source_target_pairs={{0,12},{4,0},{8,4},{12,8},{1,13},{5,1},{9,5},{13,9},{2,14},{6,2},{... | collective-permute-start | bytes 1572872 | tf_op jit(solution)/shard_map/ppermute | solution.py:55
  134.6 11.0 %collective-permute-start.24 = (bf16[1024,256]{1,0:T(8,128)(2,1)}, bf16[1024,256]{1,0:T(8,128)(2,1)}, u32[]{:S(2)}, u32[]{:S(2)}) collective-permute-start(bf16[1024,256]{1,0:T(8,128)(2,1)} %constant_dynamic-update-slice_fusion.14), channel_id=1, source_target_pairs={{0,48},{16,0},{32,16},{48,32},{1,49},{17,1},{33,17},{49,33},{2,50}... | collective-permute-start | bytes 1572872 | tf_op jit(solution)/shard_map/ppermute | solution.py:55
  135.3 10.2 %collective-permute-start.25 = (bf16[1024,256]{1,0:T(8,128)(2,1)}, bf16[1024,256]{1,0:T(8,128)(2,1)S(1)}, u32[]{:S(2)}, u32[]{:S(2)}) collective-permute-start(bf16[1024,256]{1,0:T(8,128)(2,1)} %constant_dynamic-update-slice_fusion.14), channel_id=1, source_target_pairs={{0,16},{16,32},{32,48},{48,0},{1,17},{17,33},{33,49},{49,1},{2,18}... | collective-permute-start | bytes 1572872 | tf_op jit(solution)/shard_map/ppermute | solution.py:55
  141.7 10.3 %collective-permute-start.18 = (bf16[512,256]{1,0:T(8,128)(2,1)S(1)}, bf16[512,256]{1,0:T(8,128)(2,1)S(1)}, u32[]{:S(2)}, u32[]{:S(2)}) collective-permute-start(bf16[512,256]{1,0:T(8,128)(2,1)S(1)} %slice.792), channel_id=1, source_target_pairs={{0,4},{4,8},{8,12},{12,0},{1,5},{5,9},{9,13},{13,1},{2,6},{6,10},{... | collective-permute-start | bytes 786440 | tf_op jit(solution)/shard_map/ppermute | solution.py:55
  145.5 18.4 %collective-permute-start.26 = (bf16[512,256]{1,0:T(8,128)(2,1)S(1)}, bf16[512,256]{1,0:T(8,128)(2,1)S(1)}, u32[]{:S(2)}, u32[]{:S(2)}) collective-permute-start(bf16[512,256]{1,0:T(8,128)(2,1)S(1)} %slice.798), channel_id=1, source_target_pairs={{0,16},{16,32},{32,48},{48,0},{1,17},{17,33},{33,49},{49,1},{2,18}... | collective-permute-start | bytes 786440 | tf_op jit(solution)/shard_map/ppermute | solution.py:55
  146.6 25.0 %collective-permute-start.27 = (bf16[512,256]{1,0:T(8,128)(2,1)S(1)}, bf16[512,256]{1,0:T(8,128)(2,1)S(1)}, u32[]{:S(2)}, u32[]{:S(2)}) collective-permute-start(bf16[512,256]{1,0:T(8,128)(2,1)S(1)} %slice.805), channel_id=1, source_target_pairs={{0,48},{16,0},{32,16},{48,32},{1,49},{17,1},{33,17},{49,33},{2,50}... | collective-permute-start | bytes 786440 | tf_op jit(solution)/shard_map/ppermute | solution.py:55
  153.2 26.7 %collective-permute-start.28 = (bf16[4096,256]{1,0:T(8,128)(2,1)S(1)}, bf16[4096,256]{1,0:T(8,128)(2,1)}, u32[]{:S(2)}, u32[]{:S(2)}) collective-permute-start(bf16[4096,256]{1,0:T(8,128)(2,1)S(1)} %constant_dynamic-update-slice_fusion.5), channel_id=1, source_target_pairs={{0,2},{2,0},{1,3},{3,1},{4,6},{6,4},{5,7},{7,5},{8,10},{10,8},{9,1... | collective-permute-start | bytes 6291464 | tf_op jit(solution)/shard_map/ppermute | solution.py:55
  260.1 44.6 %collective-permute-start.38 = (bf16[128,1152]{1,0:T(8,128)(2,1)}, bf16[128,1152]{1,0:T(8,128)(2,1)}, u32[]{:S(2)}, u32[]{:S(2)}) collective-permute-start(bf16[128,1152]{1,0:T(8,128)(2,1)} %slice.821), channel_id=1, source_target_pairs={{0,2},{2,0},{1,3},{3,1},{4,6},{6,4},{5,7},{7,5},{8,10},{10,8},{9,1... | collective-permute-start | bytes 884744 | tf_op jit(solution)/shard_map/ppermute | solution.py:55
  267.4 53.7 %collective-permute-start.75 = (bf16[144,2688]{1,0:T(8,128)(2,1)}, bf16[144,2688]{1,0:T(8,128)(2,1)}, u32[]{:S(2)}, u32[]{:S(2)}) collective-permute-start(bf16[144,2688]{1,0:T(8,128)(2,1)} %get-tuple-element.101), channel_id=1, source_target_pairs={{0,4},{4,8},{8,12},{12,0},{1,5},{5,9},{9,13},{13,1},{2,6},{6,10},{... | collective-permute-start | bytes 2322440 | tf_op jit(solution)/shard_map/ppermute | solution.py:55
  272.2 51.7 %collective-permute-start.77 = (bf16[144,2688]{1,0:T(8,128)(2,1)}, bf16[144,2688]{1,0:T(8,128)(2,1)}, u32[]{:S(2)}, u32[]{:S(2)}) collective-permute-start(bf16[144,2688]{1,0:T(8,128)(2,1)} %get-tuple-element.102), channel_id=1, source_target_pairs={{0,12},{4,0},{8,4},{12,8},{1,13},{5,1},{9,5},{13,9},{2,14},{6,2},{... | collective-permute-start | bytes 2322440 | tf_op jit(solution)/shard_map/ppermute | solution.py:55
  282.3 46.9 %collective-permute-start.83 = (bf16[144,2688]{1,0:T(8,128)(2,1)}, bf16[144,2688]{1,0:T(8,128)(2,1)}, u32[]{:S(2)}, u32[]{:S(2)}) collective-permute-start(bf16[144,2688]{1,0:T(8,128)(2,1)} %get-tuple-element.107), channel_id=1, source_target_pairs={{0,16},{16,32},{32,48},{48,0},{1,17},{17,33},{33,49},{49,1},{2,18}... | collective-permute-start | bytes 2322440 | tf_op jit(solution)/shard_map/ppermute | solution.py:55
  282.3 50.0 %collective-permute-start.85 = (bf16[144,2688]{1,0:T(8,128)(2,1)}, bf16[144,2688]{1,0:T(8,128)(2,1)}, u32[]{:S(2)}, u32[]{:S(2)}) collective-permute-start(bf16[144,2688]{1,0:T(8,128)(2,1)} %get-tuple-element.108), channel_id=1, source_target_pairs={{0,48},{16,0},{32,16},{48,32},{1,49},{17,1},{33,17},{49,33},{2,50}... | collective-permute-start | bytes 2322440 | tf_op jit(solution)/shard_map/ppermute | solution.py:55
  317.9 17.2 %collective-permute-start.40 = (bf16[128,1152]{1,0:T(8,128)(2,1)S(1)}, bf16[128,1152]{1,0:T(8,128)(2,1)S(1)}, u32[]{:S(2)}, u32[]{:S(2)}) collective-permute-start(bf16[128,1152]{1,0:T(8,128)(2,1)S(1)} %fusion.55), channel_id=1, source_target_pairs={{0,2},{2,0},{1,3},{3,1},{4,6},{6,4},{5,7},{7,5},{8,10},{10,8},{9,1... | collective-permute-start | bytes 884744 | tf_op jit(solution)/shard_map/ppermute | solution.py:55
  323.8 46.1 %collective-permute-start.76 = (bf16[288,2688]{1,0:T(8,128)(2,1)}, bf16[288,2688]{1,0:T(8,128)(2,1)}, u32[]{:S(2)}, u32[]{:S(2)}) collective-permute-start(bf16[288,2688]{1,0:T(8,128)(2,1)} %pad_maximum_fusion.1), channel_id=1, source_target_pairs={{0,4},{4,8},{8,12},{12,0},{1,5},{5,9},{9,13},{13,1},{2,6},{6,10},{... | collective-permute-start | bytes 4644872 | tf_op jit(solution)/shard_map/ppermute | solution.py:55
  327.1 43.1 %collective-permute-start.78 = (bf16[288,2688]{1,0:T(8,128)(2,1)}, bf16[288,2688]{1,0:T(8,128)(2,1)}, u32[]{:S(2)}, u32[]{:S(2)}) collective-permute-start(bf16[288,2688]{1,0:T(8,128)(2,1)} %pad_maximum_fusion.2), channel_id=1, source_target_pairs={{0,12},{4,0},{8,4},{12,8},{1,13},{5,1},{9,5},{13,9},{2,14},{6,2},{... | collective-permute-start | bytes 4644872 | tf_op jit(solution)/shard_map/ppermute | solution.py:55
  331.8 42.7 %collective-permute-start.84 = (bf16[288,2688]{1,0:T(8,128)(2,1)}, bf16[288,2688]{1,0:T(8,128)(2,1)}, u32[]{:S(2)}, u32[]{:S(2)}) collective-permute-start(bf16[288,2688]{1,0:T(8,128)(2,1)} %pad_maximum_fusion.3), channel_id=1, source_target_pairs={{0,16},{16,32},{32,48},{48,0},{1,17},{17,33},{33,49},{49,1},{2,18}... | collective-permute-start | bytes 4644872 | tf_op jit(solution)/shard_map/ppermute | solution.py:55
  350.6 13.1 %collective-permute-start.64 = (f32[256]{0:T(256)}, f32[256]{0:T(256)}, u32[]{:S(2)}, u32[]{:S(2)}) collective-permute-start(f32[256]{0:T(256)} %get-tuple-element.63), channel_id=1, source_target_pairs={{0,1},{1,0},{2,3},{3,2},{4,5},{5,4},{6,7},{7,6},{8,9},{9,8},{10,11... | collective-permute-start | bytes 3080 | tf_op jit(solution)/shard_map/ppermute | solution.py:55
  355.6 12.4 %collective-permute-start.41 = (bf16[128,1152]{1,0:T(8,128)(2,1)}, bf16[128,1152]{1,0:T(8,128)(2,1)}, u32[]{:S(2)}, u32[]{:S(2)}) collective-permute-start(bf16[128,1152]{1,0:T(8,128)(2,1)} %slice.823), channel_id=1, source_target_pairs={{0,2},{2,0},{1,3},{3,1},{4,6},{6,4},{5,7},{7,5},{8,10},{10,8},{9,1... | collective-permute-start | bytes 884744 | tf_op jit(solution)/shard_map/ppermute | solution.py:55
  363.7 36.3 %collective-permute-start.86 = (bf16[288,2688]{1,0:T(8,128)(2,1)}, bf16[288,2688]{1,0:T(8,128)(2,1)S(1)}, u32[]{:S(2)}, u32[]{:S(2)}) collective-permute-start(bf16[288,2688]{1,0:T(8,128)(2,1)} %pad_maximum_fusion.4), channel_id=1, source_target_pairs={{0,48},{16,0},{32,16},{48,32},{1,49},{17,1},{33,17},{49,33},{2,50}... | collective-permute-start | bytes 4644872 | tf_op jit(solution)/shard_map/ppermute | solution.py:55
  367.9 69.6 %collective-permute-start.43 = (bf16[4096,256]{0,1:T(8,128)(2,1)}, bf16[4096,256]{0,1:T(8,128)(2,1)S(1)}, u32[]{:S(2)}, u32[]{:S(2)}) collective-permute-start(bf16[4096,256]{0,1:T(8,128)(2,1)} %convolution_convert_fusion), channel_id=1, source_target_pairs={{0,2},{2,0},{1,3},{3,1},{4,6},{6,4},{5,7},{7,5},{8,10},{10,8},{9,1... | collective-permute-start | bytes 6291464 | tf_op jit(solution)/shard_map/ppermute | solution.py:55
  370.0 72.0 %collective-permute-start.52 = (bf16[4096,256]{1,0:T(8,128)(2,1)}, bf16[4096,256]{1,0:T(8,128)(2,1)S(1)}, u32[]{:S(2)}, u32[]{:S(2)}) collective-permute-start(bf16[4096,256]{1,0:T(8,128)(2,1)} %convolution_convert_fusion.2), channel_id=1, source_target_pairs={{0,2},{2,0},{1,3},{3,1},{4,6},{6,4},{5,7},{7,5},{8,10},{10,8},{9,1... | collective-permute-start | bytes 6291464 | tf_op jit(solution)/shard_map/ppermute | solution.py:55
  370.2 157.8 %collective-permute-start.42 = (bf16[128,1152]{1,0:T(8,128)(2,1)}, bf16[128,1152]{1,0:T(8,128)(2,1)}, u32[]{:S(2)}, u32[]{:S(2)}) collective-permute-start(bf16[128,1152]{1,0:T(8,128)(2,1)} %add_convert_fusion.16), channel_id=1, source_target_pairs={{0,1},{1,0},{2,3},{3,2},{4,5},{5,4},{6,7},{7,6},{8,9},{9,8},{10,11... | collective-permute-start | bytes 884744 | tf_op jit(solution)/shard_map/ppermute | solution.py:55
  374.5 29.0 %collective-permute-start.81 = (bf16[32,2688]{1,0:T(8,128)(2,1)S(1)}, bf16[32,2688]{1,0:T(8,128)(2,1)S(1)}, u32[]{:S(2)}, u32[]{:S(2)}) collective-permute-start(bf16[32,2688]{1,0:T(8,128)(2,1)S(1)} %get-tuple-element.100), channel_id=1, source_target_pairs={{0,48},{16,0},{32,16},{48,32},{1,49},{17,1},{33,17},{49,33},{2,50}... | collective-permute-start | bytes 516104 | tf_op jit(solution)/shard_map/ppermute | solution.py:55
  415.0 10.1 %collective-permute-start.80 = (bf16[72,2688]{1,0:T(8,128)(2,1)S(1)}, bf16[72,2688]{1,0:T(8,128)(2,1)S(1)}, u32[]{:S(2)}, u32[]{:S(2)}) collective-permute-start(bf16[72,2688]{1,0:T(8,128)(2,1)S(1)} %pad_maximum_fusion.16), channel_id=1, source_target_pairs={{0,16},{16,32},{32,48},{48,0},{1,17},{17,33},{33,49},{49,1},{2,18}... | collective-permute-start | bytes 1161224 | tf_op jit(solution)/shard_map/ppermute | solution.py:55
  434.6 40.5 %collective-permute-start.91 = (bf16[36,5376]{1,0:T(8,128)(2,1)}, bf16[36,5376]{1,0:T(8,128)(2,1)}, u32[]{:S(2)}, u32[]{:S(2)}) collective-permute-start(bf16[36,5376]{1,0:T(8,128)(2,1)} %pad_maximum_fusion.15), channel_id=1, source_target_pairs={{0,64},{64,0},{1,65},{65,1},{2,66},{66,2},{3,67},{67,3},{4,68},{68... | collective-permute-start | bytes 1161224 | tf_op jit(solution)/shard_map/ppermute | solution.py:55
  439.3 27.5 %collective-permute-start.44 = (bf16[512,256]{0,1:T(8,128)(2,1)}, bf16[512,256]{0,1:T(8,128)(2,1)}, u32[]{:S(2)}, u32[]{:S(2)}) collective-permute-start(bf16[512,256]{0,1:T(8,128)(2,1)} %get-tuple-element.81), channel_id=1, source_target_pairs={{0,4},{4,8},{8,12},{12,0},{1,5},{5,9},{9,13},{13,1},{2,6},{6,10},{... | collective-permute-start | bytes 786440 | tf_op jit(solution)/shard_map/ppermute | solution.py:55
  439.3 30.2 %collective-permute-start.46 = (bf16[512,256]{0,1:T(8,128)(2,1)}, bf16[512,256]{0,1:T(8,128)(2,1)}, u32[]{:S(2)}, u32[]{:S(2)}) collective-permute-start(bf16[512,256]{0,1:T(8,128)(2,1)} %get-tuple-element.82), channel_id=1, source_target_pairs={{0,12},{4,0},{8,4},{12,8},{1,13},{5,1},{9,5},{13,9},{2,14},{6,2},{... | collective-permute-start | bytes 786440 | tf_op jit(solution)/shard_map/ppermute | solution.py:55
  451.3 19.7 %collective-permute-start.53 = (bf16[512,256]{0,1:T(8,128)(2,1)}, bf16[512,256]{0,1:T(8,128)(2,1)}, u32[]{:S(2)}, u32[]{:S(2)}) collective-permute-start(bf16[512,256]{0,1:T(8,128)(2,1)} %copy.106), channel_id=1, source_target_pairs={{0,16},{16,32},{32,48},{48,0},{1,17},{17,33},{33,49},{49,1},{2,18}... | collective-permute-start | bytes 786440 | tf_op jit(solution)/shard_map/ppermute | solution.py:55
  470.8 17.4 %collective-permute-start.45 = (bf16[1024,256]{0,1:T(8,128)(2,1)S(1)}, bf16[1024,256]{0,1:T(8,128)(2,1)S(1)}, u32[]{:S(2)}, u32[]{:S(2)}) collective-permute-start(bf16[1024,256]{0,1:T(8,128)(2,1)S(1)} %pad_maximum_fusion.11), channel_id=1, source_target_pairs={{0,4},{4,8},{8,12},{12,0},{1,5},{5,9},{9,13},{13,1},{2,6},{6,10},{... | collective-permute-start | bytes 1572872 | tf_op jit(solution)/shard_map/ppermute | solution.py:55
  471.0 17.3 %collective-permute-start.47 = (bf16[1024,256]{0,1:T(8,128)(2,1)S(1)}, bf16[1024,256]{0,1:T(8,128)(2,1)S(1)}, u32[]{:S(2)}, u32[]{:S(2)}) collective-permute-start(bf16[1024,256]{0,1:T(8,128)(2,1)S(1)} %pad_maximum_fusion.12), channel_id=1, source_target_pairs={{0,12},{4,0},{8,4},{12,8},{1,13},{5,1},{9,5},{13,9},{2,14},{6,2},{... | collective-permute-start | bytes 1572872 | tf_op jit(solution)/shard_map/ppermute | solution.py:55
  474.8 16.5 %collective-permute-start.54 = (bf16[1024,256]{0,1:T(8,128)(2,1)S(1)}, bf16[1024,256]{0,1:T(8,128)(2,1)S(1)}, u32[]{:S(2)}, u32[]{:S(2)}) collective-permute-start(bf16[1024,256]{0,1:T(8,128)(2,1)S(1)} %pad_maximum_fusion.13), channel_id=1, source_target_pairs={{0,16},{16,32},{32,48},{48,0},{1,17},{17,33},{33,49},{49,1},{2,18}... | collective-permute-start | bytes 1572872 | tf_op jit(solution)/shard_map/ppermute | solution.py:55
  484.5 13.9 %collective-permute-start.56 = (bf16[1024,256]{0,1:T(8,128)(2,1)S(1)}, bf16[1024,256]{0,1:T(8,128)(2,1)S(1)}, u32[]{:S(2)}, u32[]{:S(2)}) collective-permute-start(bf16[1024,256]{0,1:T(8,128)(2,1)S(1)} %pad_maximum_fusion.14), channel_id=1, source_target_pairs={{0,48},{16,0},{32,16},{48,32},{1,49},{17,1},{33,17},{49,33},{2,50}... | collective-permute-start | bytes 1572872 | tf_op jit(solution)/shard_map/ppermute | solution.py:55
  488.6 12.9 %collective-permute-start.48 = (bf16[128,256]{0,1:T(8,128)(2,1)S(1)}, bf16[128,256]{0,1:T(8,128)(2,1)S(1)}, u32[]{:S(2)}, u32[]{:S(2)}) collective-permute-start(bf16[128,256]{0,1:T(8,128)(2,1)S(1)} %get-tuple-element.120), channel_id=1, source_target_pairs={{0,16},{16,32},{32,48},{48,0},{1,17},{17,33},{33,49},{49,1},{2,18}... | collective-permute-start | bytes 196616 | tf_op jit(solution)/shard_map/ppermute | solution.py:55
  488.7 12.8 %collective-permute-start.50 = (bf16[128,256]{0,1:T(8,128)(2,1)S(1)}, bf16[128,256]{0,1:T(8,128)(2,1)S(1)}, u32[]{:S(2)}, u32[]{:S(2)}) collective-permute-start(bf16[128,256]{0,1:T(8,128)(2,1)S(1)} %get-tuple-element.121), channel_id=1, source_target_pairs={{0,48},{16,0},{32,16},{48,32},{1,49},{17,1},{33,17},{49,33},{2,50}... | collective-permute-start | bytes 196616 | tf_op jit(solution)/shard_map/ppermute | solution.py:55
  521.2 13.0 %collective-permute-start.63 = (bf16[128,256]{0,1:T(8,128)(2,1)}, bf16[128,256]{0,1:T(8,128)(2,1)}, u32[]{:S(2)}, u32[]{:S(2)}) collective-permute-start(bf16[128,256]{0,1:T(8,128)(2,1)} %broadcast_select_fusion.2), channel_id=1, source_target_pairs={{0,2},{2,0},{1,3},{3,1},{4,6},{6,4},{5,7},{7,5},{8,10},{10,8},{9,1... | collective-permute-start | bytes 196616 | tf_op jit(solution)/shard_map/ppermute | solution.py:55
  537.5 13.5 %collective-permute-start.65 = (bf16[144,896]{0,1:T(8,128)(2,1)S(1)}, bf16[144,896]{0,1:T(8,128)(2,1)S(1)}, u32[]{:S(2)}, u32[]{:S(2)}) collective-permute-start(bf16[144,896]{0,1:T(8,128)(2,1)S(1)} %get-tuple-element.93), channel_id=1, source_target_pairs={{0,4},{4,8},{8,12},{12,0},{1,5},{5,9},{9,13},{13,1},{2,6},{6,10},{... | collective-permute-start | bytes 774152 | tf_op jit(solution)/shard_map/ppermute | solution.py:55
  537.5 13.5 %collective-permute-start.67 = (bf16[144,896]{0,1:T(8,128)(2,1)S(1)}, bf16[144,896]{0,1:T(8,128)(2,1)S(1)}, u32[]{:S(2)}, u32[]{:S(2)}) collective-permute-start(bf16[144,896]{0,1:T(8,128)(2,1)S(1)} %get-tuple-element.94), channel_id=1, source_target_pairs={{0,12},{4,0},{8,4},{12,8},{1,13},{5,1},{9,5},{13,9},{2,14},{6,2},{... | collective-permute-start | bytes 774152 | tf_op jit(solution)/shard_map/ppermute | solution.py:55
  553.7 14.3 %collective-permute-start.66 = (bf16[288,896]{1,0:T(8,128)(2,1)}, bf16[288,896]{1,0:T(8,128)(2,1)}, u32[]{:S(2)}, u32[]{:S(2)}) collective-permute-start(bf16[288,896]{1,0:T(8,128)(2,1)} %copy.79), channel_id=1, source_target_pairs={{0,4},{4,8},{8,12},{12,0},{1,5},{5,9},{9,13},{13,1},{2,6},{6,10},{... | collective-permute-start | bytes 1548296 | tf_op jit(solution)/shard_map/ppermute | solution.py:55
  557.2 12.5 %collective-permute-start.68 = (bf16[288,896]{1,0:T(8,128)(2,1)}, bf16[288,896]{1,0:T(8,128)(2,1)}, u32[]{:S(2)}, u32[]{:S(2)}) collective-permute-start(bf16[288,896]{1,0:T(8,128)(2,1)} %copy.81), channel_id=1, source_target_pairs={{0,12},{4,0},{8,4},{12,8},{1,13},{5,1},{9,5},{13,9},{2,14},{6,2},{... | collective-permute-start | bytes 1548296 | tf_op jit(solution)/shard_map/ppermute | solution.py:55
  (184 other events, 1477.9 us)
Sparse Core Ops, SparseCore 0:
  26.4 105.7 all-gather.1
